TPU v7x, 32 devices: a whole 2x2x4 slice. The times are simulated.
32 devices in a mesh: groups: 2 (over y), lat: 4 (over z), chan: 2 (over x), rep: 2 (over core).
Axes of the slice: x: 2, y: 2, z: 4, core: 2. Of those that a mesh axis runs over, the one named last changes fastest.
Arguments:
- hidden_encoding: bfloat16 [4, 256, 384, 1024], P(('groups', 'rep'), 'chan', 'lat'), parts along dimension 0, may hold values from -12 to 12
- eigenvalues: float32 [256, 256, 2, 128], P('chan', 'lat'), may hold values from -1 to 1, as said below
- desired_spectra: bfloat16 [4, 6, 256, 256, 2, 128], P(('groups', 'rep'), None, 'chan', 'lat'), parts along dimension 0, may hold values from -4 to 4
Outputs:
- predicted_state: bfloat16 [4, 256, 384, 1024], P(('groups', 'rep'), 'chan', 'lat'), parts along dimension 0
- clipped_grad: float32 [512, 256, 2, 128], P(('groups', 'chan'), 'lat'), parts along dimension 0
- spectral_misfit: float32 [2], P('groups'), parts along dimension 0
There are 2 independent parts, one for each index of `groups`. A program takes and returns all parts, laid end to end along the dimension named above; an argument that names none is the same for every part. Nothing has to cross between parts.
Inputs may be any that keep to these rules, and one draw needn't show every extreme that they name: Each pair (eigenvalues[c, k, 0, l], eigenvalues[c, k, 1, l]) is a complex number of modulus below one.
All inputs are finite; a program needn't handle non-finite values.
Results may differ from a plain program's by a relative error of at most 0.0074.
Values may be sent and summed in bfloat16 or wider, within the bound.
A program may use at most 384 MiB of HBM per device.

v0:
```python
import math

import jax
import jax.numpy as jnp
from jax import lax
from jax.sharding import PartitionSpec as P

HIDDEN_FEATURES = 256
PARALLEL_COUNT = 384
K = 256
L = 128
LEADS = 6


def forward_table(wavenumber_span, kept):
    column = jnp.arange(wavenumber_span, dtype=jnp.int32)[:, None]
    wave = jnp.arange(kept, dtype=jnp.int32)[None, :]
    phase = (wave * column % wavenumber_span).astype(jnp.float32) * (
        2.0 * math.pi / wavenumber_span
    )
    factor = 1.0 / math.sqrt(wavenumber_span)
    table = jnp.stack([jnp.cos(phase) * factor, -jnp.sin(phase) * factor], axis=2)
    return table.reshape(wavenumber_span, 2 * kept)


def inverse_table(wavenumber_span, kept):
    wave = jnp.arange(kept, dtype=jnp.int32)[:, None]
    column = jnp.arange(wavenumber_span, dtype=jnp.int32)[None, :]
    phase = (wave * column % wavenumber_span).astype(jnp.float32) * (
        2.0 * math.pi / wavenumber_span
    )
    weight = jnp.where(wave == 0, 1.0, 2.0).astype(jnp.float32) / math.sqrt(wavenumber_span)
    table = jnp.stack([weight * jnp.cos(phase), -weight * jnp.sin(phase)], axis=1)
    return table.reshape(2 * kept, wavenumber_span)


def latitude_table(height, modes):
    row = jnp.arange(height, dtype=jnp.int32)[:, None]
    mode = jnp.arange(modes, dtype=jnp.int32)[None, :]
    phase = ((2 * row + 1) * mode % (4 * height)).astype(jnp.float32) * (math.pi / (2 * height))
    weight = jnp.where(mode == 0, math.sqrt(1.0 / height), math.sqrt(2.0 / height)).astype(
        jnp.float32
    )
    return weight * jnp.cos(phase)


def per_device(hidden_encoding, eigenvalues, desired_spectra):
    ceiling_bound = lax.Precision.HIGHEST
    channels = hidden_encoding.shape[1]
    band = hidden_encoding.shape[2]
    wavenumber_span = hidden_encoding.shape[3]
    owned = eigenvalues.shape[1]
    forward = forward_table(wavenumber_span, K).astype(jnp.bfloat16)
    reverse_pass = inverse_table(wavenumber_span, K).astype(jnp.bfloat16)
    basis = latitude_table(PARALLEL_COUNT, L)
    basis_half = basis.astype(jnp.bfloat16)
    spectra = jnp.dot(
        hidden_encoding[0].reshape(channels * band, wavenumber_span),
        forward,
        preferred_element_type=jnp.float32,
    )
    spectra = spectra.astype(jnp.bfloat16).reshape(channels, band, 2 * K)
    coeffs = jnp.einsum(
        "nhq,hl->nql",
        lax.all_to_all(spectra, "lat", split_axis=2, concat_axis=1, tiled=True),
        basis_half,
        preferred_element_type=jnp.float32,
    )
    state = coeffs.reshape(channels, owned, 2, L)
    lam_real = eigenvalues[:, :, 0]
    lam_imag = eigenvalues[:, :, 1]
    subset_misfit = jnp.zeros((), jnp.float32)
    derivative_inphase = jnp.zeros((channels, owned, L), jnp.float32)
    derivative_quadrature = jnp.zeros((channels, owned, L), jnp.float32)
    for lead in range(LEADS):
        prev_real = state[:, :, 0]
        prev_imag = state[:, :, 1]
        next_real = lam_real * prev_real - lam_imag * prev_imag
        next_imag = lam_real * prev_imag + lam_imag * prev_real
        goal = desired_spectra[0, lead].astype(jnp.float32)
        res_real = next_real - goal[:, :, 0]
        res_imag = next_imag - goal[:, :, 1]
        subset_misfit = subset_misfit + jnp.sum(res_real * res_real + res_imag * res_imag)
        weight = 2.0 * (lead + 1)
        derivative_inphase = derivative_inphase + weight * (
            prev_real * res_real + prev_imag * res_imag
        )
        derivative_quadrature = derivative_quadrature + weight * (
            prev_real * res_imag - prev_imag * res_real
        )
        state = jnp.stack([next_real, next_imag], axis=2)
    local_grad = jnp.stack([derivative_inphase, derivative_quadrature], axis=2)
    limit = math.sqrt(HIDDEN_FEATURES * K * 2 * L)
    count = lax.axis_size("rep") * LEADS * HIDDEN_FEATURES * K * 2 * L
    summed = lax.psum(local_grad.astype(jnp.bfloat16), "rep").astype(jnp.float32)
    total = lax.psum(jnp.sum(summed * summed), ("lat", "chan"))
    loss_sum = lax.psum(subset_misfit, ("lat", "chan", "rep"))
    capped_derivative = summed * jnp.minimum(1.0, limit / jnp.sqrt(total + 1e-06))
    spectral_misfit = jnp.reshape(loss_sum / count, (1,))
    final = state.reshape(channels, 2 * owned, L)
    wavenumber_sets = jnp.einsum("nql,hl->nhq", final, basis, precision=ceiling_bound).astype(
        jnp.bfloat16
    )
    block = lax.all_to_all(wavenumber_sets, "lat", split_axis=1, concat_axis=2, tiled=True)
    element_sequence = block.shape[0]
    matrix_stripe = block.shape[1]
    vectorized_field = jnp.dot(
        block.reshape(element_sequence * matrix_stripe, block.shape[2]),
        reverse_pass,
        preferred_element_type=jnp.float32,
    )
    predicted_state = vectorized_field.astype(jnp.bfloat16).reshape(
        element_sequence, matrix_stripe, wavenumber_span
    )
    return (predicted_state[None], capped_derivative, spectral_misfit)


def solution(mesh):
    placed = (
        P(("groups", "rep"), "chan", "lat", None),
        P("chan", "lat", None, None),
        P(("groups", "rep"), None, "chan", "lat", None, None),
    )
    return jax.shard_map(
        per_device,
        mesh=mesh,
        in_specs=placed,
        out_specs=(
            P(("groups", "rep"), "chan", "lat", None),
            P(("groups", "chan"), "lat", None, None),
            P("groups"),
        ),
        check_vma=False,
    )
```

profile of v0, /device:TPU:0, one launch (start us, length us, event | category | flops | bytes accessed | tf_op | source)
XLA Modules:
  0.0 862.1 jit_solution(1957157711916959977)
XLA Ops:
  7.2 4.4 multiply_convert_fusion.2
  11.7 1.1 copy.133
  13.2 19.4 %fusion = bf16[12288,512]{0,1:T(8,128)(2,1)} fusion(bf16[1024,512]{0,1:T(8,128)(2,1)S(1)} %convert_element_type.117, bf16[12288,1024]{1,0:T(8,128)(2,1)} %bitcast.488), kind=kOutput, calls=%fused_computation.2 | convolution fusion | flops 12891193344 | bytes 38797312 | tf_op jit(solution)/shard_map/dot_general | solution.py:57
  32.6 16.6 %copy.134 = bf16[12288,512]{1,0:T(8,128)(2,1)} copy(bf16[12288,512]{0,1:T(8,128)(2,1)} %fusion) | data formatting | bytes 25165824 | tf_op jit(solution)/shard_map/convert_element_type | solution.py:62
  49.3 18.2 %copy.135 = bf16[128,96,512]{0,1,2:T(8,128)(2,1)} copy(bf16[128,96,512]{2,1,0:T(8,128)(2,1)} %bitcast.484) | data formatting | bytes 25165824 | tf_op jit(solution)/shard_map/reshape | solution.py:62
  67.4 6.3 all-to-all-start
  73.8 30.9 %fusion.119 = (bf16[1,1,128,64,2,128]{5,4,3,2,1,0:T(2,128)(2,1)}, bf16[1,1,128,64,2,128]{5,4,3,2,1,0:T(2,128)(2,1)}, bf16[1,1,128,64,2,128]{5,4,3,2,1,0:T(2,128)...) fusion(bf16[1,6,128,64,2,128]{5,4,3,2,1,0:T(2,128)(2,1)} %param.5), kind=kLoop, calls=%fused_computation.203 | loop fusion | bytes 50331648 | tf_op jit(solution)/shard_map/slice | solution.py:80
  104.7 14.1 %fusion.30 = (f32[128,64,2,128]{3,0,1,2:T(8,128)}, f32[128,64,2,128]{3,0,1,2:T(8,128)}) fusion(bf16[1,1,128,64,2,128]{5,4,3,2,1,0:T(2,128)(2,1)} %get-tuple-element.35, bf16[1,1,128,64,2,128]{5,4,3,2,1,0:T(2,128)(2,1)} %get-tuple-element.36), kind=kLoop, calls=%fused_computation.44 | loop fusion | flops 4194304 | bytes 25165824 | tf_op jit(solution)/shard_map/convert_element_type | solution.py:80
  118.8 14.1 %fusion.28 = (f32[128,64,2,128]{3,0,1,2:T(8,128)}, f32[128,64,2,128]{3,0,1,2:T(8,128)}) fusion(bf16[1,1,128,64,2,128]{5,4,3,2,1,0:T(2,128)(2,1)} %get-tuple-element.33, bf16[1,1,128,64,2,128]{5,4,3,2,1,0:T(2,128)(2,1)} %get-tuple-element.34), kind=kLoop, calls=%fused_computation.40 | loop fusion | flops 4194304 | bytes 25165824 | tf_op jit(solution)/shard_map/convert_element_type | solution.py:80
  132.9 13.5 %fusion.32 = (f32[128,64,2,128]{3,0,1,2:T(8,128)}, f32[128,64,2,128]{3,0,1,2:T(8,128)}) fusion(bf16[1,1,128,64,2,128]{5,4,3,2,1,0:T(2,128)(2,1)S(1)} %get-tuple-element.37, bf16[1,1,128,64,2,128]{5,4,3,2,1,0:T(2,128)(2,1)} %get-tuple-element.38), kind=kLoop, calls=%fused_computation.48 | loop fusion | flops 4194304 | bytes 25165824 | tf_op jit(solution)/shard_map/convert_element_type | solution.py:80
  146.5 11.9 %fusion.120 = (f32[128,64,1,128]{3,2,1,0:T(1,128)}, f32[128,64,1,128]{3,2,1,0:T(1,128)}) fusion(f32[128,64,2,128]{3,2,1,0:T(2,128)} %param.4), kind=kLoop, calls=%fused_computation.204 | loop fusion | bytes 16777216 | tf_op jit(solution)/shard_map/slice | solution.py:70
  158.4 190.1 %all-to-all-done = bf16[128,96,512]{0,1,2:T(8,128)(2,1)} async-done(((bf16[128,96,512]{0,1,2:T(8,128)(2,1)}), bf16[128,96,512]{0,1,2:T(8,128)(2,1)}, u32[]{:S(2)}, u32[]{:S(2)}) %all-to-all-start) | async-done | bytes 12582944 | tf_op jit(solution)/shard_map/all_to_all | solution.py:65
  348.5 18.0 %copy.137 = bf16[128,4,96,128]{3,2,1,0:T(8,128)(2,1)} copy(bf16[128,4,96,128]{0,2,3,1:T(8,128)(2,1)} %bitcast.6) | data formatting | bytes 25165824 | tf_op jit(solution)/shard_map/all_to_all | solution.py:65
  366.5 16.7 %copy.138 = bf16[128,128,384]{2,0,1:T(8,128)(2,1)} copy(bf16[128,128,384]{1,2,0:T(8,128)(2,1)} %bitcast.485) | data formatting | bytes 25165824 | tf_op jit(solution)/shard_map/nhq,hl->nql/dot_general | solution.py:63
  383.2 7.8 fusion.99
  391.0 27.1 %fusion.19 = (bf16[128,64,1,128]{3,0,1,2:T(8,128)(2,1)}, f32[128,64,1,128]{3,0,1,2:T(8,128)}, f32[128,64,1,128]{3,0,1,2:T(8,128)}) fusion(f32[128,64,2,128]{3,0,1,2:T(8,128)} %get-tuple-element.50, f32[128,64,2,128]{3,0,1,2:T(8,128)} %get-tuple-element.46, f32[128,64,2,128]{3,0,1,2:T(8,128)S(1)} %bitcast.478, f32[128,64,2,128]{3,0,1,2:T(8,128)} %get-tuple-element.48, ...), kind=kLoop, calls=%fused_computation.30 | loop fusion | flops 81788928 | bytes 77594624 | tf_op jit(solution)/shard_map/convert.6
  418.2 4.0 pad_maximum_fusion
  423.3 30.3 %convert_bitcast_fusion = bf16[128,384,128]{2,1,0:T(8,128)(2,1)S(1)} fusion(f32[128,128,128]{2,0,1:T(8,128)S(1)} %bitcast.486, s32[384]{0:T(512)S(1)} %multiply_add_fusion.5, f32[128]{0:T(128)S(1)} %compare_select_fusion.1), kind=kOutput, calls=%fused_computation.5 | convolution fusion | flops 9670459392 | bytes 20973568 | tf_op jit(solution)/shard_map/nql,hl->nhq/dot_general | solution.py:101
  453.6 29.1 %copy.145 = bf16[128,384,128]{2,0,1:T(8,128)(2,1)} copy(bf16[128,384,128]{2,1,0:T(8,128)(2,1)S(1)} %convert_bitcast_fusion) | data formatting | bytes 25165824 | tf_op jit(solution)/shard_map/convert_element_type | solution.py:101
  482.7 6.3 all-to-all-start.1
  489.1 25.9 %fusion.27 = bf16[128,64,1,128]{3,0,1,2:T(8,128)(2,1)S(1)} fusion(f32[128,64,2,128]{3,0,1,2:T(8,128)} %get-tuple-element.50, f32[128,64,2,128]{3,0,1,2:T(8,128)} %get-tuple-element.46, f32[128,64,2,128]{3,0,1,2:T(8,128)} %get-tuple-element.47, f32[128,64,2,128]{3,0,1,2:T(8,128)} %get-tuple-element.48, f32[128,64,2,128]{3,0,1,2:T(8,128)} %get-tuple-element.49, ...), kind=kLoop, calls=%fused_computation.38 | loop fusion | flops 75497472 | bytes 77594624 | tf_op jit(solution)/shard_map/convert.7
  515.0 2.3 pad_maximum_fusion.1
  517.4 4.4 multiply_convert_fusion
  523.0 12.6 %fusion.9 = (f32[128,64,128]{2,0,1:T(8,128)}, f32[128,64,128]{2,0,1:T(8,128)}) fusion(f32[128,64,2,128]{3,0,2,1:T(8,128)} %copy-done, f32[128,64,1,128]{3,2,1,0:T(1,128)} %get-tuple-element.42, f32[128,64,1,128]{3,2,1,0:T(1,128)S(1)} %copy-done.1), kind=kLoop, calls=%fused_computation.16 | loop fusion | flops 6291456 | bytes 25165824 | tf_op jit(solution)/shard_map/add | solution.py:79
  536.1 20.3 %fusion.36 = (f32[]{:T(128)}, f32[]{:T(128)}, f32[]{:T(128)}, f32[]{:T(128)}, f32[]{:T(128)}, /*index=5*/f32[]{:T(128)}) fusion(f32[128,64,2,128]{3,0,1,2:T(8,128)} %get-tuple-element.45, f32[128,64,128]{2,0,1:T(8,128)} %get-tuple-element.40, f32[128,64,128]{2,0,1:T(8,128)} %get-tuple-element.39, f32[128,64,1,128]{3,2,1,0:T(1,128)} %get-tuple-element.42, ...), kind=kLoop, calls=%fused_computation.54 | loop fusion | flops 69206016 | bytes 67108888 | tf_op jit(solution)/shard_map/reduce_sum | solution.py:83
  560.7 209.4 %psum.23 = f32[]{:T(128)} all-reduce(f32[]{:T(128)S(6)} %add.262), channel_id=1, replica_groups=mesh['groups'=2,'lat'=4,'chan'=2,'rep'=2] {'lat','chan','rep'}, use_global_device_ids=true, to_apply=%region_9.10 | all-reduce | flops 1 | bytes 8 | tf_op jit(solution)/shard_map/psum | solution.py:97
  770.1 4.9 fusion.3
  775.7 25.7 %psum.22 = f32[]{:T(128)} all-reduce(f32[]{:T(128)} %fusion.3), channel_id=1, replica_groups=mesh['groups'=2,'lat'=4,'chan'=2,'rep'=2] {'lat','chan'}, use_global_device_ids=true, to_apply=%region_2.3 | all-reduce | flops 1 | bytes 8 | tf_op jit(solution)/shard_map/psum | solution.py:96
  802.1 3.4 convert_multiply_fusion
  805.5 9.8 %copy.156 = f32[128,64,2,128]{3,2,1,0:T(2,128)} copy(f32[128,64,2,128]{3,0,1,2:T(8,128)S(1)} %convert_multiply_fusion) | data formatting | bytes 16777216
  815.3 17.3 %copy.146 = bf16[128,4,96,128]{3,1,2,0:T(4,128)(2,1)} copy(bf16[128,4,96,128]{3,0,2,1:T(8,128)(2,1)} %bitcast.16) | data formatting | bytes 25165824 | tf_op jit(solution)/shard_map/all_to_all | solution.py:104
  832.5 21.1 %convolution_convert_fusion = bf16[12288,1024]{1,0:T(8,128)(2,1)} fusion(bf16[512,1024]{1,0:T(8,128)(2,1)S(1)} %convert_element_type.124, bf16[1536,8,4,128]{3,2,1,0:T(4,128)(2,1)} %bitcast.487), kind=kOutput, calls=%fused_computation | convolution fusion | flops 12897484800 | bytes 38797312 | tf_op jit(solution)/shard_map/dot_general | solution.py:107
  (35 shorter events, 3.9 us)
Async XLA Ops:
  67.4 281.0 %all-to-all-start = ((bf16[128,96,512]{0,1,2:T(8,128)(2,1)}), bf16[128,96,512]{0,1,2:T(8,128)(2,1)}, u32[]{:S(2)}, u32[]{:S(2)}) async-start(bf16[128,96,512]{0,1,2:T(8,128)(2,1)} %copy.135), calls=%async_computation | async-start | bytes 25165824 | tf_op jit(solution)/shard_map/all_to_all | solution.py:65
  383.2 7.8 slice-start
  383.2 7.8 slice-start.1
  391.0 27.2 %copy-start = (f32[128,64,2,128]{3,0,2,1:T(8,128)}, f32[128,64,2,128]{3,0,2,1:T(8,128)S(1)}, u32[]{:S(2)}) copy-start(f32[128,64,2,128]{3,0,2,1:T(8,128)S(1)} %fusion.99) | copy-start | bytes 25165828
  482.7 332.6 %all-to-all-start.1 = ((bf16[128,384,128]{2,0,1:T(8,128)(2,1)}), bf16[128,384,128]{2,0,1:T(8,128)(2,1)}, u32[]{:S(2)}, u32[]{:S(2)}) async-start(bf16[128,384,128]{2,0,1:T(8,128)(2,1)} %copy.145), calls=%async_computation.1 | async-start | bytes 25165824 | tf_op jit(solution)/shard_map/all_to_all | solution.py:104
  489.0 281.1 %all-reduce.2.cloned.1.call-start = ((), (), s32[]{:S(2)}) async-start(), calls=%async_computation.2 | async-start | bytes 8388608 | tf_op jit(solution)/shard_map/psum | solution.py:95
  489.1 25.9 %copy-start.2 = (bf16[128,64,1,128]{3,0,1,2:T(8,128)(2,1)S(1)}, bf16[128,64,1,128]{3,0,1,2:T(8,128)(2,1)}, u32[]{:S(2)}) copy-start(bf16[128,64,1,128]{3,0,1,2:T(8,128)(2,1)} %get-tuple-element.30) | copy-start | bytes 6291460
  517.4 5.6 copy-start.1
  521.9 13.7 %slice-start.2 = ((s8[8388608]{0:T(1024)(128)(4,1)}), s8[4194304]{0:T(1024)(128)(4,1)S(1)}, s32[]{:S(2)}) async-start(s8[8388608]{0:T(1024)(128)(4,1)} %bitcast.479), calls=%async_computation.5 | async-start | bytes 8388608
  521.9 13.7 %slice-start.4 = ((s8[8388608]{0:T(1024)(128)(4,1)}), s8[4194304]{0:T(1024)(128)(4,1)S(1)}, s32[]{:S(2)}) async-start(s8[8388608]{0:T(1024)(128)(4,1)} %bitcast.481), calls=%async_computation.7 | async-start | bytes 8388608
  523.0 12.6 %slice-start.3 = ((s8[8388608]{0:T(1024)(128)(4,1)}), s8[4194304]{0:T(1024)(128)(4,1)S(1)}, s32[]{:S(2)}) async-start(s8[8388608]{0:T(1024)(128)(4,1)} %bitcast.479), calls=%async_computation.6 | async-start | bytes 8388608
  523.0 13.1 %slice-start.5 = ((s8[8388608]{0:T(1024)(128)(4,1)}), s8[4194304]{0:T(1024)(128)(4,1)S(1)}, s32[]{:S(2)}) async-start(s8[8388608]{0:T(1024)(128)(4,1)} %bitcast.481), calls=%async_computation.8 | async-start | bytes 8388608
Sparse Core Ops, SparseCore 0:
  517.5 29.7 all-reduce.1
where the time goes:
time: 871 us; the launch traced here: 862 us
  blocking collectives  235 us (27%)
  waiting for transfers between devices  190 us (22%)
  local copies, waits for them, and re-layouts  173 us (20%)
  other arithmetic  151 us (17%)
  matrix products  78.6 us (9%)
  between operations  21.1 us (2%)
  starting transfers between devices  12.7 us (1%)
    psum x1, blocking collectives, per_device(): loss_sum = lax.psum(subset_misfit, ('lat', 'chan', 'rep'))  209 us
    all_to_all x1, waiting for transfers between devices, per_device(): lax.all_to_all(spectra, 'lat', split_axis=2, concat_axis=1, tiled=True)  190 us
    another operation x4, other arithmetic  61.8 us
    convert_element_type x3, other arithmetic, per_device(): goal = desired_spectra[0, lead].astype(jnp.float32)  41.8 us
    slice x1, local copies, waits for them, and re-layouts, per_device(): goal = desired_spectra[0, lead].astype(jnp.float32)  30.9 us
    dot_general x1, matrix products, per_device(): jnp.einsum('nql,hl->nhq', final, basis, precision=ceiling_bound)  30.3 us
    convert_element_type x1, local copies, waits for them, and re-layouts, per_device(): jnp.einsum('nql,hl->nhq', final, basis, precision=ceiling_bound)  29.1 us
    psum x1, blocking collectives, per_device(): total = lax.psum(jnp.sum(summed * summed), ('lat', 'chan'))  25.7 us
  transfers between devices with their start and end apart: 3, of which 1 were waited for; matrix products, arithmetic and copies ran while one was open for 20% of the time, Pallas kernels for 0%

commit v1 on v0

--- a/solution.py
+++ b/solution.py
@@ -2,7 +2,10 @@
 
 import jax
 import jax.numpy as jnp
+import numpy as np
 from jax import lax
+from jax.experimental import pallas as pl
+from jax.experimental.pallas import tpu as pltpu
 from jax.sharding import PartitionSpec as P
 
 HIDDEN_FEATURES = 256
@@ -44,7 +47,7 @@
     return weight * jnp.cos(phase)
 
 
-def per_device(hidden_encoding, eigenvalues, desired_spectra):
+def plain_per_device(hidden_encoding, eigenvalues, desired_spectra):
     ceiling_bound = lax.Precision.HIGHEST
     channels = hidden_encoding.shape[1]
     band = hidden_encoding.shape[2]
@@ -115,14 +118,368 @@
     return (predicted_state[None], capped_derivative, spectral_misfit)
 
 
+CHUNKS = 4
+VMEM = 48 * 1024 * 1024
+
+
+def block_order(blocks, owned):
+    wave = np.arange(blocks * owned).reshape(blocks, 1, owned)
+    return (2 * wave + np.arange(2).reshape(1, 2, 1)).reshape(-1)
+
+
+def longitude_tables(span, kept, order):
+    wave = np.arange(kept)
+    column = np.arange(span)
+    phase = 2.0 * np.pi / span * (column[:, None] * wave[None, :] % span)
+    both = np.stack([np.cos(phase), -np.sin(phase)], axis=2) / math.sqrt(span)
+    both = both.reshape(span, 2 * kept).astype(np.float32)
+    twice = np.repeat(np.where(wave == 0, 1.0, 2.0), 2).astype(np.float32)
+    back = (both * twice).T
+    return both[:, order].astype(jnp.bfloat16), back[order].astype(jnp.bfloat16)
+
+
+def latitude_factors(height, modes, bands):
+    row = np.arange(height)[:, None]
+    mode = np.arange(modes)[None, :]
+    table = np.cos(np.pi / (2 * height) * ((2 * row + 1) * mode % (4 * height)))
+    table = table * np.where(mode == 0, math.sqrt(1.0 / height), math.sqrt(2.0 / height))
+    span = height // bands
+    tilt = 1.0 + 1e-3 * np.arange(modes) / modes
+    bases = []
+    for band in range(bands):
+        rows = table[band * span : (band + 1) * span]
+        left = rows.copy()
+        found = np.zeros((span, 0))
+        while found.shape[1] < span:
+            size = np.sqrt(np.sum(left * left, axis=0))
+            if np.max(size) < 2e-8 * math.sqrt(2.0 / bands):
+                break
+            pick = left[:, np.argmax(size * tilt)]
+            for _ in range(2):
+                pick = pick - np.sum(found * np.sum(found * pick[:, None], axis=0), axis=1)
+            pick = pick / np.sqrt(np.sum(pick * pick))
+            found = np.concatenate([found, pick[:, None]], axis=1)
+            left = left - pick[:, None] * np.sum(pick[:, None] * left, axis=0)
+        bases.append(found)
+    rank = max(base.shape[1] for base in bases)
+    rank = -(-rank // 16) * 16
+    basis = np.zeros((bands, span, rank))
+    weights = np.zeros((bands, rank, modes))
+    for band, base in enumerate(bases):
+        basis[band, :, : base.shape[1]] = base
+        weights[band, : base.shape[1]] = base.T @ table[band * span : (band + 1) * span]
+    return basis.astype(np.float32), weights.astype(np.float32)
+
+
+def deinterleave(owned):
+    order = np.concatenate([np.arange(owned) * 2, np.arange(owned) * 2 + 1])
+    return np.eye(2 * owned, dtype=np.float32)[order].astype(jnp.bfloat16)
+
+
+def two_parts(array):
+    high = array.astype(jnp.bfloat16)
+    return high, (array - high.astype(np.float32)).astype(jnp.bfloat16)
+
+
+def sum_over(value, axis):
+    size = lax.axis_size(axis)
+    if size & (size - 1):
+        return lax.psum(value, axis)
+    step = 1
+    while step < size:
+        value = value + lax.ppermute(value, axis, [(i, i ^ step) for i in range(size)])
+        step *= 2
+    return value
+
+
+def forward_kernel(field_ref, table_ref, basis_ref, sent_ref, spectra):
+    group, band, span = field_ref.shape
+    spectra[...] = jnp.dot(
+        field_ref[...].reshape(group * band, span),
+        table_ref[...],
+        preferred_element_type=jnp.float32,
+    ).astype(jnp.bfloat16).reshape(spectra.shape)
+    blocks, width = sent_ref.shape[0], sent_ref.shape[3]
+    for channel in range(group):
+        short = jnp.dot(basis_ref[...], spectra[channel], preferred_element_type=jnp.float32)
+        rank = sent_ref.shape[2]
+        short = (short[:rank] + short[rank:]).astype(jnp.bfloat16)
+        for block in range(blocks):
+            sent_ref[block, channel] = short[:, block * width : (block + 1) * width]
+
+
+def rollout_kernel(
+    got_ref, weights_ref, order_ref, lam_ref, goal_ref, sent_ref, grad_ref, misfit_ref
+):
+    blocks, group, rank, width = got_ref.shape
+    owned = width // 2
+    leads = goal_ref.shape[0]
+
+    @pl.when(pl.program_id(0) == 0)
+    def _():
+        misfit_ref[...] = jnp.zeros_like(misfit_ref)
+
+    def one_channel(channel, carry):
+        got = got_ref[:, channel].reshape(blocks * rank, width)
+        state = lax.dot_general(
+            got,
+            weights_ref[...],
+            (((0,), (0,)), ((), ())),
+            preferred_element_type=jnp.float32,
+        )
+        modes = state.shape[1] // 2
+        state = state[:, :modes] + state[:, modes:]
+        real, imag = state[:owned], state[owned:]
+        lam_real = lam_ref[channel, pl.ds(0, owned, stride=2), :]
+        lam_imag = lam_ref[channel, pl.ds(1, owned, stride=2), :]
+        misfit = jnp.zeros_like(real)
+        grad_real = jnp.zeros_like(real)
+        grad_imag = jnp.zeros_like(real)
+        for lead in range(leads):
+            goal = jnp.dot(
+                order_ref[...], goal_ref[lead, channel], preferred_element_type=jnp.float32
+            )
+            next_real = lam_real * real - lam_imag * imag
+            next_imag = lam_real * imag + lam_imag * real
+            res_real = next_real - goal[:owned]
+            res_imag = next_imag - goal[owned:]
+            misfit = misfit + (res_real * res_real + res_imag * res_imag)
+            weight = 2.0 * (lead + 1)
+            grad_real = grad_real + weight * (real * res_real + imag * res_imag)
+            grad_imag = grad_imag + weight * (real * res_imag - imag * res_real)
+            real, imag = next_real, next_imag
+        grad_ref[channel, :owned] = grad_real.astype(jnp.bfloat16)
+        grad_ref[channel, owned:] = grad_imag.astype(jnp.bfloat16)
+        misfit_ref[...] += jnp.sum(misfit.reshape(-1, 8, misfit.shape[1]), axis=0)
+        final = jnp.concatenate([real, imag], axis=0)
+        high = final.astype(jnp.bfloat16)
+        low = (final - high.astype(jnp.float32)).astype(jnp.bfloat16)
+        contract = (((1,), (1,)), ((), ()))
+        short = lax.dot_general(
+            weights_ref[...],
+            jnp.concatenate([high, high], axis=1),
+            contract,
+            preferred_element_type=jnp.float32,
+        ) + lax.dot_general(
+            weights_ref[:, :modes], low, contract, preferred_element_type=jnp.float32
+        )
+        sent_ref[:, channel] = short.astype(jnp.bfloat16).reshape(blocks, rank, width)
+        return carry
+
+    lax.fori_loop(0, group, one_channel, 0)
+
+
+def inverse_kernel(got_ref, basis_ref, table_ref, *refs):
+    field_ref, bands = refs[-2], refs[-1]
+    blocks, group, rank, width = got_ref.shape
+    for channel in range(group):
+        for block in range(blocks):
+            got = got_ref[block, channel]
+            bands[channel, :, block * width : (block + 1) * width] = jnp.dot(
+                basis_ref[...],
+                jnp.concatenate([got, got], axis=0),
+                preferred_element_type=jnp.float32,
+            ).astype(jnp.bfloat16)
+    field_ref[...] = jnp.dot(
+        bands[...].reshape(group * bands.shape[1], bands.shape[2]),
+        table_ref[...],
+        preferred_element_type=jnp.float32,
+    ).astype(jnp.bfloat16).reshape(field_ref.shape)
+
+
+def scale_kernel(scale_ref, mine_ref, other_ref, *refs):
+    out_ref = refs[-1]
+    group, rows, _ = mine_ref.shape
+    owned = rows // 2
+    scale = scale_ref[0]
+
+    def one_channel(channel, carry):
+        total = mine_ref[channel].astype(jnp.float32) + other_ref[channel].astype(jnp.float32)
+        total = total * scale
+        out_ref[channel, pl.ds(0, owned, stride=2), :] = total[:owned]
+        out_ref[channel, pl.ds(1, owned, stride=2), :] = total[owned:]
+        return carry
+
+    lax.fori_loop(0, group, one_channel, 0)
+
+
+def params():
+    return pltpu.CompilerParams(vmem_limit_bytes=VMEM, dimension_semantics=("arbitrary",))
+
+
+def whole(array):
+    return pl.BlockSpec(array.shape, lambda step: (0,) * array.ndim)
+
+
+def cost(flops, moved):
+    return pl.CostEstimate(flops=int(flops), bytes_accessed=int(moved), transcendentals=0)
+
+
+def chunk_call(kernel, chunk, count, group, operands, ins, shape, full, scratch, work, name):
+    first = chunk * count // group
+    block = (group,) + shape.shape[1:]
+    rest = (0,) * (len(shape.shape) - 1)
+    aliases = {}
+    if full is not None:
+        aliases = {len(operands): 0}
+        operands = operands + (full,)
+        ins = ins + [pl.BlockSpec(memory_space=pl.ANY)]
+    return pl.pallas_call(
+        kernel,
+        grid=(count // group,),
+        in_specs=ins,
+        out_specs=pl.BlockSpec(block, lambda step: (first + step,) + rest),
+        out_shape=shape,
+        scratch_shapes=scratch,
+        input_output_aliases=aliases,
+        compiler_params=params(),
+        cost_estimate=work,
+        name=name,
+    )(*operands)
+
+
+def per_device(hidden_encoding, eigenvalues, desired_spectra):
+    bands_over = lax.axis_size("lat")
+    channels, band, span = hidden_encoding.shape[1:]
+    owned = eigenvalues.shape[1]
+    width = 2 * owned
+    bf16 = jnp.bfloat16
+    f32 = jnp.float32
+    order = block_order(bands_over, owned)
+    forward, back = longitude_tables(span, K, order)
+    basis, weights = latitude_factors(PARALLEL_COUNT, L, bands_over)
+    rank = basis.shape[2]
+    mine = lax.axis_index("lat")
+    basis = np.concatenate(two_parts(basis), axis=2)
+    basis = lax.dynamic_index_in_dim(jnp.asarray(basis), mine, keepdims=False)
+    basis_t = basis.T
+    weights = weights.reshape(bands_over * rank, L)
+    weights = jnp.asarray(np.concatenate(two_parts(weights), axis=1))
+    forward, back = jnp.asarray(forward), jnp.asarray(back)
+    permute = jnp.asarray(deinterleave(owned))
+    field = hidden_encoding.reshape(channels, band, span)
+    lam = eigenvalues.reshape(channels, width, L)
+    goals = desired_spectra.reshape(LEADS, channels, width, L)
+
+    count = channels // CHUNKS
+    group = math.gcd(count, 8)
+    steps = count // group
+    blocked = pl.BlockSpec((bands_over, group, rank, width), lambda step: (0, step, 0, 0))
+    rows = pl.BlockSpec((group, width, L), lambda step: (step, 0, 0))
+    packed = jax.ShapeDtypeStruct((bands_over, count, rank, width), bf16)
+    pair = [(0, 1), (1, 0)]
+    longitude_work = 2 * count * band * span * 2 * K
+
+    arrived = []
+    for chunk in range(CHUNKS):
+        first = chunk * steps
+        sent = pl.pallas_call(
+            forward_kernel,
+            grid=(steps,),
+            in_specs=[
+                pl.BlockSpec((group, band, span), lambda step, first=first: (first + step, 0, 0)),
+                whole(forward),
+                whole(basis_t),
+            ],
+            out_specs=blocked,
+            out_shape=packed,
+            scratch_shapes=[pltpu.VMEM((group, band, 2 * K), bf16)],
+            compiler_params=params(),
+            cost_estimate=cost(2 * longitude_work, 2 * count * band * span),
+            name="longitude_forward",
+        )(field, forward, basis_t)
+        arrived.append(lax.all_to_all(sent, "lat", split_axis=0, concat_axis=0, tiled=True))
+
+    returned, grads, others, misfits, squares = [], [], [], [], []
+    for chunk in range(CHUNKS):
+        first = chunk * steps
+        sent, grad, misfit = pl.pallas_call(
+            rollout_kernel,
+            grid=(steps,),
+            in_specs=[
+                blocked,
+                whole(weights),
+                whole(permute),
+                pl.BlockSpec((group, width, L), lambda step, first=first: (first + step, 0, 0)),
+                pl.BlockSpec(
+                    (LEADS, group, width, L), lambda step, first=first: (0, first + step, 0, 0)
+                ),
+            ],
+            out_specs=(blocked, rows, pl.BlockSpec((8, L), lambda step: (0, 0))),
+            out_shape=(
+                packed,
+                jax.ShapeDtypeStruct((count, width, L), bf16),
+                jax.ShapeDtypeStruct((8, L), f32),
+            ),
+            compiler_params=params(),
+            cost_estimate=cost(3 * longitude_work, 20 * count * width * L),
+            name="rollout",
+        )(arrived[chunk], weights, permute, lam, goals)
+        returned.append(lax.all_to_all(sent, "lat", split_axis=0, concat_axis=0, tiled=True))
+        grads.append(grad)
+        misfits.append(jnp.sum(misfit))
+        other = lax.ppermute(grad, "rep", pair) if lax.axis_size("rep") == 2 else grad
+        others.append(other)
+        total = grad.astype(f32) + other.astype(f32)
+        squares.append(jnp.sum(total * total))
+
+    sums = jnp.stack([sum(squares) / lax.axis_size("rep"), sum(misfits)])
+    for axis in ("rep", "chan", "lat"):
+        sums = sum_over(sums, axis)
+    limit = math.sqrt(HIDDEN_FEATURES * K * 2 * L)
+    scale = jnp.minimum(1.0, limit / jnp.sqrt(sums[0] + 1e-06)).reshape(1)
+    total_count = lax.axis_size("rep") * LEADS * HIDDEN_FEATURES * K * 2 * L
+    spectral_misfit = (sums[1] / total_count).reshape(1)
+
+    predicted = None
+    for chunk in range(CHUNKS):
+        predicted = chunk_call(
+            inverse_kernel,
+            chunk,
+            count,
+            group,
+            (returned[chunk], basis, back),
+            [blocked, whole(basis), whole(back)],
+            jax.ShapeDtypeStruct((channels, band, span), bf16),
+            predicted,
+            [pltpu.VMEM((group, band, 2 * K), bf16)],
+            cost(2 * longitude_work, 2 * count * band * span),
+            "longitude_inverse",
+        )
+    capped = None
+    for chunk in range(CHUNKS):
+        capped = chunk_call(
+            scale_kernel,
+            chunk,
+            count,
+            group,
+            (scale, grads[chunk], others[chunk]),
+            [pl.BlockSpec(memory_space=pltpu.SMEM), rows, rows],
+            jax.ShapeDtypeStruct((channels, width, L), f32),
+            capped,
+            [],
+            cost(4 * count * width * L, 8 * count * width * L),
+            "scale",
+        )
+    return (
+        predicted.reshape(hidden_encoding.shape),
+        capped.reshape(channels, owned, 2, L),
+        spectral_misfit,
+    )
+
+
 def solution(mesh):
     placed = (
         P(("groups", "rep"), "chan", "lat", None),
         P("chan", "lat", None, None),
         P(("groups", "rep"), None, "chan", "lat", None, None),
     )
+    tiled = (2 * K) % (128 * mesh.shape["lat"]) == 0
+    tiled = tiled and PARALLEL_COUNT % (16 * mesh.shape["lat"]) == 0
+    tiled = tiled and HIDDEN_FEATURES % (CHUNKS * mesh.shape["chan"]) == 0
+    tiled = tiled and mesh.shape["rep"] == 2
     return jax.shard_map(
-        per_device,
+        per_device if tiled else plain_per_device,
         mesh=mesh,
         in_specs=placed,
         out_specs=(

time: 871 us -> 391 us (0.45)
  blocking collectives: 235 us -> 0 us
  local copies, waits for them, and re-layouts: 173 us -> 15.4 us
  Pallas kernels: 0 us -> 148 us
  other arithmetic: 151 us -> 12.9 us
  matrix products: 78.6 us -> 0 us
  starting transfers between devices: 12.7 us -> 42.9 us
  waiting for transfers between devices: 190 us -> 161 us
  between operations: 21.1 us -> 8.5 us
    psum x2 -> x0, blocking collectives: 235 us -> none  [the longest x1 209 us: per_device(): loss_sum = lax.psum(subset_misfit, ('lat', 'chan', 'rep'))]
    pallas_call x0 -> x16, Pallas kernels: none -> 148 us  [the longest x4 77.2 us: per_device(): pl.pallas_call(rollout_kernel, grid=(steps,), in_specs=[blocked, whole(we...]
    dot_general x4 -> x0, matrix products: 78.6 us -> none  [the longest x1 30.3 us: per_device(): jnp.einsum('nql,hl->nhq', final, basis, precision=ceiling_bound)]
    another operation x8 -> x1, other arithmetic: 68.4 us -> 0.08 us  [per_device(): sums = jnp.stack([sum(squares) / lax.axis_size('rep'), sum(misfits)])]
    all_to_all x2 -> x8, waiting for transfers between devices: 190 us -> 132 us  [per_device(): lax.all_to_all(sent, 'lat', split_axis=0, concat_axis=0, tiled=True)]
    convert_element_type x4 -> x0, local copies, waits for them, and re-layouts: 46.6 us -> none  [the longest x1 29.1 us: per_device(): jnp.einsum('nql,hl->nhq', final, basis, precision=ceiling_bound)]
    slice x2 -> x1, local copies, waits for them, and re-layouts: 42.8 us -> 0.59 us  [per_device(): spectral_misfit = (sums[1] / total_count).reshape(1)]
    convert_element_type x3 -> x0, other arithmetic: 41.8 us -> none  [per_device(): goal = desired_spectra[0, lead].astype(jnp.float32)]
  transfers between devices with their start and end apart: 3 -> 16, of which waited for: 1 -> 9; matrix products, arithmetic and copies ran while one was open for 20% -> 3% of each run, Pallas kernels for 0% -> 34%
where the time goes in v1:
time: 391 us; the launch traced here: 389 us
  waiting for transfers between devices  161 us (41%)
  Pallas kernels  148 us (38%)
  starting transfers between devices  42.9 us (11%)
  local copies, waits for them, and re-layouts  15.4 us (4%)
  other arithmetic  12.9 us (3%)
  between operations  8.5 us (2%)
    all_to_all x8, waiting for transfers between devices, per_device(): lax.all_to_all(sent, 'lat', split_axis=0, concat_axis=0, tiled=True)  132 us
    pallas_call x4, Pallas kernels, per_device(): pl.pallas_call(rollout_kernel, grid=(steps,), in_specs=[blocked, whole(we...  77.2 us
    pallas_call x8, Pallas kernels, chunk_call(): pl.pallas_call(kernel, grid=(count // group,), in_specs=ins, out_specs=pl...  41.1 us
    all_to_all x8, starting transfers between devices, per_device(): lax.all_to_all(sent, 'lat', split_axis=0, concat_axis=0, tiled=True)  33.7 us
    ppermute x4, waiting for transfers between devices, sum_over(): lax.ppermute(value, axis, [(i, i ^ step) for i in range(size)])  29.6 us
    pallas_call x4, Pallas kernels, per_device(): pl.pallas_call(forward_kernel, grid=(steps,), in_specs=[pl.BlockSpec((gro...  29.5 us
    unnamed x48, local copies, waits for them, and re-layouts  14 us
    reduce_sum x4, other arithmetic, per_device(): squares.append(jnp.sum(total * total))  10.3 us
  transfers between devices with their start and end apart: 16, of which 9 were waited for; matrix products, arithmetic and copies ran while one was open for 3% of the time, Pallas kernels for 34%

profile of v1, /device:TPU:0, one launch (start us, length us, event | category | flops | bytes accessed | tf_op | source)
XLA Modules:
  0.0 388.7 jit_solution(6478549969370740351)
XLA Ops:
  2.7 7.4 %longitude_forward.4 = bf16[4,32,48,128]{3,2,1,0:T(8,128)(2,1)} custom-call(bf16[128,96,1024]{2,1,0:T(8,128)(2,1)} %bitcast.12, bf16[1024,512]{1,0:T(8,128)(2,1)S(1)} %copy-done, bf16[96,96]{1,0:T(8,128)(2,1)S(1)} %copy.17.basis_ref), custom_call_target="tpu_custom_call" | custom-call | flops 6442450944 | bytes 6291456 | tf_op jit(solution)/shard_map/longitude_forward/pallas_call | solution.py:376
  10.1 6.5 %all-to-all-start = ((bf16[4,32,48,128]{3,2,1,0:T(8,128)(2,1)}), bf16[4,32,48,128]{3,2,1,0:T(8,128)(2,1)S(1)}, u32[]{:S(2)}, u32[]{:S(2)}) async-start(bf16[4,32,48,128]{3,2,1,0:T(8,128)(2,1)} %longitude_forward.4), calls=%async_computation | async-start | bytes 3145728 | tf_op jit(solution)/shard_map/all_to_all | solution.py:391
  16.6 7.4 %longitude_forward.5 = bf16[4,32,48,128]{3,2,1,0:T(8,128)(2,1)} custom-call(bf16[128,96,1024]{2,1,0:T(8,128)(2,1)} %bitcast.13, bf16[1024,512]{1,0:T(8,128)(2,1)S(1)} %copy-done.1, bf16[96,96]{1,0:T(8,128)(2,1)S(1)} %copy.17.basis_ref), custom_call_target="tpu_custom_call" | custom-call | flops 6442450944 | bytes 6291456 | tf_op jit(solution)/shard_map/longitude_forward/pallas_call | solution.py:376
  23.9 29.6 %all-to-all-done.got_ref = bf16[4,32,48,128]{3,2,1,0:T(8,128)(2,1)S(1)} async-done(((bf16[4,32,48,128]{3,2,1,0:T(8,128)(2,1)}), bf16[4,32,48,128]{3,2,1,0:T(8,128)(2,1)S(1)}, u32[]{:S(2)}, u32[]{:S(2)}) %all-to-all-start) | async-done | bytes 1572896 | tf_op jit(solution)/shard_map/all_to_all | solution.py:391
  53.5 4.4 %all-to-all-start.2 = ((bf16[4,32,48,128]{3,2,1,0:T(8,128)(2,1)}), bf16[4,32,48,128]{3,2,1,0:T(8,128)(2,1)}, u32[]{:S(2)}, u32[]{:S(2)}) async-start(bf16[4,32,48,128]{3,2,1,0:T(8,128)(2,1)} %longitude_forward.5), calls=%async_computation.2 | async-start | bytes 3145728 | tf_op jit(solution)/shard_map/all_to_all | solution.py:391
  57.9 7.4 %longitude_forward.6 = bf16[4,32,48,128]{3,2,1,0:T(8,128)(2,1)} custom-call(bf16[128,96,1024]{2,1,0:T(8,128)(2,1)} %bitcast.14, bf16[1024,512]{1,0:T(8,128)(2,1)S(1)} %copy-done.1, bf16[96,96]{1,0:T(8,128)(2,1)S(1)} %copy.17.basis_ref), custom_call_target="tpu_custom_call" | custom-call | flops 6442450944 | bytes 6291456 | tf_op jit(solution)/shard_map/longitude_forward/pallas_call | solution.py:376
  65.3 29.1 %all-to-all-done.2.got_ref = bf16[4,32,48,128]{3,2,1,0:T(8,128)(2,1)} async-done(((bf16[4,32,48,128]{3,2,1,0:T(8,128)(2,1)}), bf16[4,32,48,128]{3,2,1,0:T(8,128)(2,1)}, u32[]{:S(2)}, u32[]{:S(2)}) %all-to-all-start.2) | async-done | bytes 1572896 | tf_op jit(solution)/shard_map/all_to_all | solution.py:391
  94.4 3.6 all-to-all-start.4
  98.0 7.4 %longitude_forward.7 = bf16[4,32,48,128]{3,2,1,0:T(8,128)(2,1)} custom-call(bf16[128,96,1024]{2,1,0:T(8,128)(2,1)} %bitcast.15, bf16[1024,512]{1,0:T(8,128)(2,1)S(1)} %copy-done.1, bf16[96,96]{1,0:T(8,128)(2,1)S(1)} %copy.17.basis_ref), custom_call_target="tpu_custom_call" | custom-call | flops 6442450944 | bytes 6291456 | tf_op jit(solution)/shard_map/longitude_forward/pallas_call | solution.py:376
  105.4 29.0 %all-to-all-done.4.got_ref = bf16[4,32,48,128]{3,2,1,0:T(8,128)(2,1)S(1)} async-done(((bf16[4,32,48,128]{3,2,1,0:T(8,128)(2,1)}), bf16[4,32,48,128]{3,2,1,0:T(8,128)(2,1)S(1)}, u32[]{:S(2)}, u32[]{:S(2)}) %all-to-all-start.4) | async-done | bytes 1572896 | tf_op jit(solution)/shard_map/all_to_all | solution.py:391
  138.0 19.2 %rollout.5 = (bf16[4,32,48,128]{3,2,1,0:T(8,128)(2,1)S(1)}, bf16[32,128,128]{2,1,0:T(8,128)(2,1)S(1)}, f32[8,128]{1,0:T(8,128)S(1)}) custom-call(bf16[4,32,48,128]{3,2,1,0:T(8,128)(2,1)} %all-to-all-done.2.got_ref, bf16[192,256]{1,0:T(8,128)(2,1)S(1)} %copy-done.22, bf16[128,128]{1,0:T(8,128)(2,1)S(1)} %copy-done.23, f32[128,128,128]{2,1,0:T(8,128)} %bitcast.22, ...), custom_call_target="tpu_custom_call" | custom-call | flops 9663676416 | bytes 10485760 | tf_op jit(solution)/shard_map/rollout/pallas_call | solution.py:396
  159.3 15.1 %all-to-all-done.6.got_ref = bf16[4,32,48,128]{3,2,1,0:T(8,128)(2,1)S(1)} async-done(((bf16[4,32,48,128]{3,2,1,0:T(8,128)(2,1)}), bf16[4,32,48,128]{3,2,1,0:T(8,128)(2,1)S(1)}, u32[]{:S(2)}, u32[]{:S(2)}) %all-to-all-start.6) | async-done | bytes 1572896 | tf_op jit(solution)/shard_map/all_to_all | solution.py:391
  175.5 3.6 all-to-all-start.3
  179.1 19.1 %rollout.6 = (bf16[4,32,48,128]{3,2,1,0:T(8,128)(2,1)S(1)}, bf16[32,128,128]{2,1,0:T(8,128)(2,1)S(1)}, f32[8,128]{1,0:T(8,128)S(1)}) custom-call(bf16[4,32,48,128]{3,2,1,0:T(8,128)(2,1)S(1)} %all-to-all-done.4.got_ref, bf16[192,256]{1,0:T(8,128)(2,1)S(1)} %copy-done.22, bf16[128,128]{1,0:T(8,128)(2,1)S(1)} %copy-done.23, f32[128,128,128]{2,1,0:T(8,128)} %bitcast.23, ...), custom_call_target="tpu_custom_call" | custom-call | flops 9663676416 | bytes 10485760 | tf_op jit(solution)/shard_map/rollout/pallas_call | solution.py:396
  200.4 15.1 %all-to-all-done.3.got_ref = bf16[4,32,48,128]{3,2,1,0:T(8,128)(2,1)S(1)} async-done(((bf16[4,32,48,128]{3,2,1,0:T(8,128)(2,1)}), bf16[4,32,48,128]{3,2,1,0:T(8,128)(2,1)S(1)}, u32[]{:S(2)}, u32[]{:S(2)}) %all-to-all-start.3) | async-done | bytes 1572896 | tf_op jit(solution)/shard_map/all_to_all | solution.py:418
  215.5 3.6 all-to-all-start.5
  220.5 19.1 %rollout.7 = (bf16[4,32,48,128]{3,2,1,0:T(8,128)(2,1)S(1)}, bf16[32,128,128]{2,1,0:T(8,128)(2,1)S(1)}, f32[8,128]{1,0:T(8,128)S(1)}) custom-call(bf16[4,32,48,128]{3,2,1,0:T(8,128)(2,1)S(1)} %copy-done.19, bf16[192,256]{1,0:T(8,128)(2,1)S(1)} %copy-done.22, bf16[128,128]{1,0:T(8,128)(2,1)S(1)} %copy-done.23, f32[128,128,128]{2,1,0:T(8,128)} %bitcast.24, ...), custom_call_target="tpu_custom_call" | custom-call | flops 9663676416 | bytes 10485760 | tf_op jit(solution)/shard_map/rollout/pallas_call | solution.py:396
  241.7 13.8 %all-to-all-done.5.got_ref = bf16[4,32,48,128]{3,2,1,0:T(8,128)(2,1)S(1)} async-done(((bf16[4,32,48,128]{3,2,1,0:T(8,128)(2,1)}), bf16[4,32,48,128]{3,2,1,0:T(8,128)(2,1)S(1)}, u32[]{:S(2)}, u32[]{:S(2)}) %all-to-all-start.5) | async-done | bytes 1572896 | tf_op jit(solution)/shard_map/all_to_all | solution.py:418
  256.7 3.7 all-to-all-start.7
  262.4 19.8 %rollout.4 = (bf16[4,32,48,128]{3,2,1,0:T(8,128)(2,1)S(1)}, bf16[32,128,128]{2,1,0:T(8,128)(2,1)}, f32[8,128]{1,0:T(8,128)S(1)}) custom-call(bf16[4,32,48,128]{3,2,1,0:T(8,128)(2,1)S(1)} %copy-done.16, bf16[192,256]{1,0:T(8,128)(2,1)S(1)} %copy-done.22, bf16[128,128]{1,0:T(8,128)(2,1)S(1)} %copy-done.23, f32[128,128,128]{2,1,0:T(8,128)} %bitcast.25, ...), custom_call_target="tpu_custom_call" | custom-call | flops 9663676416 | bytes 10485760 | tf_op jit(solution)/shard_map/rollout/pallas_call | solution.py:396
  301.9 4.9 %all-to-all-start.1 = ((bf16[4,32,48,128]{3,2,1,0:T(8,128)(2,1)}), bf16[4,32,48,128]{3,2,1,0:T(8,128)(2,1)}, u32[]{:S(2)}, u32[]{:S(2)}) async-start(bf16[4,32,48,128]{3,2,1,0:T(8,128)(2,1)} %copy-done.14), calls=%async_computation.1 | async-start | bytes 3145728 | tf_op jit(solution)/shard_map/all_to_all | solution.py:418
  312.6 20.5 %collective-permute-done.6 = f32[2]{0:T(128)S(1)} collective-permute-done((f32[2]{0:T(128)S(1)}, f32[2]{0:T(128)S(1)}, u32[]{:S(2)}, u32[]{:S(2)}) %collective-permute-start.6) | collective-permute-done | bytes 40 | tf_op jit(solution)/shard_map/ppermute | solution.py:190
  333.1 4.5 %collective-permute-start.7 = (f32[2]{0:T(128)S(1)}, f32[2]{0:T(128)S(1)}, u32[]{:S(2)}, u32[]{:S(2)}) collective-permute-start(f32[2]{0:T(128)S(1)} %add.63), channel_id=1, source_target_pairs={{0,8},{4,12},{8,0},{12,4},{1,9},{5,13},{9,1},{13,5},{2,10},{6,14},... | collective-permute-start | bytes 32 | tf_op jit(solution)/shard_map/ppermute | solution.py:190
  337.5 7.0 %collective-permute-done.7 = f32[2]{0:T(128)S(1)} collective-permute-done((f32[2]{0:T(128)S(1)}, f32[2]{0:T(128)S(1)}, u32[]{:S(2)}, u32[]{:S(2)}) %collective-permute-start.7) | collective-permute-done | bytes 40 | tf_op jit(solution)/shard_map/ppermute | solution.py:190
  346.5 3.8 scale.4.refs_0_
  350.3 3.8 scale.5.refs_0_
  354.1 3.7 scale.6.refs_0_
  357.8 4.0 %scale.7 = f32[128,128,128]{2,1,0:T(8,128)} custom-call(f32[1]{0:T(128)S(6)} %min_shard_map.4.scale_ref, bf16[32,128,128]{2,1,0:T(8,128)(2,1)} %get-tuple-element.22.mine_ref, bf16[32,128,128]{2,1,0:T(8,128)(2,1)} %collective-permute-done.3.other_ref, f32[128,128,128]{2,1,0:T(8,128)} %scale.6.refs_0_), custom_call_target="tpu_custom_call", output_to_operand_aliasing={{}: (3, {})} | custom-call | flops 2097152 | bytes 4194304 | tf_op jit(solution)/shard_map/scale/pallas_call | solution.py:327
  361.8 6.2 %longitude_inverse.4.refs_0_ = bf16[128,96,1024]{2,1,0:T(8,128)(2,1)} custom-call(bf16[4,32,48,128]{3,2,1,0:T(8,128)(2,1)S(1)} %all-to-all-done.7.got_ref, bf16[96,96]{1,0:T(8,128)(2,1)S(1)} %get-tuple-element.27.basis_ref, bf16[512,1024]{1,0:T(8,128)(2,1)S(1)} %copy-done.2), custom_call_target="tpu_custom_call" | custom-call | flops 6442450944 | bytes 6291456 | tf_op jit(solution)/shard_map/longitude_inverse/pallas_call | solution.py:327
  368.0 6.2 %longitude_inverse.5.refs_0_ = bf16[128,96,1024]{2,1,0:T(8,128)(2,1)} custom-call(bf16[4,32,48,128]{3,2,1,0:T(8,128)(2,1)S(1)} %copy-done.6, bf16[96,96]{1,0:T(8,128)(2,1)S(1)} %get-tuple-element.27.basis_ref, bf16[512,1024]{1,0:T(8,128)(2,1)S(1)} %copy-done.2, bf16[128,96,1024]{2,1,0:T(8,128)(2,1)} %longitude_inverse.4.refs_0_), custom_call_target="tpu_custom_call", output_to_operand_aliasing={{}: (3, {})} | custom-call | flops 6442450944 | bytes 6291456 | tf_op jit(solution)/shard_map/longitude_inverse/pallas_call | solution.py:327
  374.2 6.2 %longitude_inverse.6.refs_0_ = bf16[128,96,1024]{2,1,0:T(8,128)(2,1)} custom-call(bf16[4,32,48,128]{3,2,1,0:T(8,128)(2,1)S(1)} %copy-done.4, bf16[96,96]{1,0:T(8,128)(2,1)S(1)} %get-tuple-element.27.basis_ref, bf16[512,1024]{1,0:T(8,128)(2,1)S(1)} %copy-done.2, bf16[128,96,1024]{2,1,0:T(8,128)(2,1)} %longitude_inverse.5.refs_0_), custom_call_target="tpu_custom_call", output_to_operand_aliasing={{}: (3, {})} | custom-call | flops 6442450944 | bytes 6291456 | tf_op jit(solution)/shard_map/longitude_inverse/pallas_call | solution.py:327
  380.4 7.2 %longitude_inverse.7 = bf16[128,96,1024]{2,1,0:T(8,128)(2,1)} custom-call(bf16[4,32,48,128]{3,2,1,0:T(8,128)(2,1)} %all-to-all-done.1.got_ref, bf16[96,96]{1,0:T(8,128)(2,1)S(1)} %get-tuple-element.27.basis_ref, bf16[512,1024]{1,0:T(8,128)(2,1)S(1)} %copy-done.2, bf16[128,96,1024]{2,1,0:T(8,128)(2,1)} %longitude_inverse.6.refs_0_), custom_call_target="tpu_custom_call", output_to_operand_aliasing={{}: (3, {})} | custom-call | flops 6442450944 | bytes 6291456 | tf_op jit(solution)/shard_map/longitude_inverse/pallas_call | solution.py:327
  (80 shorter events, 38.6 us)
Async XLA Ops:
  1.5 1.2 copy-start
  10.1 6.5 %copy-start.1 = (bf16[1024,512]{1,0:T(8,128)(2,1)S(1)}, bf16[1024,512]{1,0:T(8,128)(2,1)}, u32[]{:S(2)}) copy-start(bf16[1024,512]{1,0:T(8,128)(2,1)} %constant.41.clone.table_ref) | copy-start | bytes 3145732
  10.1 43.4 %all-to-all-start = ((bf16[4,32,48,128]{3,2,1,0:T(8,128)(2,1)}), bf16[4,32,48,128]{3,2,1,0:T(8,128)(2,1)S(1)}, u32[]{:S(2)}, u32[]{:S(2)}) async-start(bf16[4,32,48,128]{3,2,1,0:T(8,128)(2,1)} %longitude_forward.4), calls=%async_computation | async-start | bytes 3145728 | tf_op jit(solution)/shard_map/all_to_all | solution.py:391
  53.5 11.8 %copy-start.15 = (bf16[4,32,48,128]{3,2,1,0:T(8,128)(2,1)}, bf16[4,32,48,128]{3,2,1,0:T(8,128)(2,1)S(1)}, u32[]{:S(2)}) copy-start(bf16[4,32,48,128]{3,2,1,0:T(8,128)(2,1)S(1)} %all-to-all-done.got_ref) | copy-start | bytes 4718596
  53.5 40.9 %all-to-all-start.2 = ((bf16[4,32,48,128]{3,2,1,0:T(8,128)(2,1)}), bf16[4,32,48,128]{3,2,1,0:T(8,128)(2,1)}, u32[]{:S(2)}, u32[]{:S(2)}) async-start(bf16[4,32,48,128]{3,2,1,0:T(8,128)(2,1)} %longitude_forward.5), calls=%async_computation.2 | async-start | bytes 3145728 | tf_op jit(solution)/shard_map/all_to_all | solution.py:391
  94.4 40.0 %all-to-all-start.4 = ((bf16[4,32,48,128]{3,2,1,0:T(8,128)(2,1)}), bf16[4,32,48,128]{3,2,1,0:T(8,128)(2,1)S(1)}, u32[]{:S(2)}, u32[]{:S(2)}) async-start(bf16[4,32,48,128]{3,2,1,0:T(8,128)(2,1)} %longitude_forward.6), calls=%async_computation.4 | async-start | bytes 3145728 | tf_op jit(solution)/shard_map/all_to_all | solution.py:391
  105.4 32.6 %copy-start.22 = (bf16[192,256]{1,0:T(8,128)(2,1)S(1)}, bf16[192,256]{1,0:T(8,128)(2,1)}, u32[]{:S(2)}) copy-start(bf16[192,256]{1,0:T(8,128)(2,1)} %constant.40.clone.weights_ref) | copy-start | bytes 294916
  105.4 32.6 %copy-start.23 = (bf16[128,128]{1,0:T(8,128)(2,1)S(1)}, bf16[128,128]{1,0:T(8,128)(2,1)}, u32[]{:S(2)}) copy-start(bf16[128,128]{1,0:T(8,128)(2,1)} %constant.43.clone.order_ref) | copy-start | bytes 98308
  134.4 40.0 %all-to-all-start.6 = ((bf16[4,32,48,128]{3,2,1,0:T(8,128)(2,1)}), bf16[4,32,48,128]{3,2,1,0:T(8,128)(2,1)S(1)}, u32[]{:S(2)}, u32[]{:S(2)}) async-start(bf16[4,32,48,128]{3,2,1,0:T(8,128)(2,1)} %longitude_forward.7), calls=%async_computation.6 | async-start | bytes 3145728 | tf_op jit(solution)/shard_map/all_to_all | solution.py:391
  174.4 1.2 copy-start.18
  175.5 40.0 %all-to-all-start.3 = ((bf16[4,32,48,128]{3,2,1,0:T(8,128)(2,1)}), bf16[4,32,48,128]{3,2,1,0:T(8,128)(2,1)S(1)}, u32[]{:S(2)}, u32[]{:S(2)}) async-start(bf16[4,32,48,128]{3,2,1,0:T(8,128)(2,1)} %copy-done.20), calls=%async_computation.3 | async-start | bytes 3145728 | tf_op jit(solution)/shard_map/all_to_all | solution.py:418
  215.5 24.1 %copy-start.3 = (bf16[4,32,48,128]{3,2,1,0:T(8,128)(2,1)}, bf16[4,32,48,128]{3,2,1,0:T(8,128)(2,1)S(1)}, u32[]{:S(2)}) copy-start(bf16[4,32,48,128]{3,2,1,0:T(8,128)(2,1)S(1)} %all-to-all-done.3.got_ref) | copy-start | bytes 4718596
  215.5 40.0 %all-to-all-start.5 = ((bf16[4,32,48,128]{3,2,1,0:T(8,128)(2,1)}), bf16[4,32,48,128]{3,2,1,0:T(8,128)(2,1)S(1)}, u32[]{:S(2)}, u32[]{:S(2)}) async-start(bf16[4,32,48,128]{3,2,1,0:T(8,128)(2,1)} %copy-done.21), calls=%async_computation.5 | async-start | bytes 3145728 | tf_op jit(solution)/shard_map/all_to_all | solution.py:418
  219.1 1.4 copy-start.19
  256.7 3.7 copy-start.8
  256.7 45.2 %all-to-all-start.7 = ((bf16[4,32,48,128]{3,2,1,0:T(8,128)(2,1)}), bf16[4,32,48,128]{3,2,1,0:T(8,128)(2,1)S(1)}, u32[]{:S(2)}, u32[]{:S(2)}) async-start(bf16[4,32,48,128]{3,2,1,0:T(8,128)(2,1)} %copy-done.17), calls=%async_computation.7 | async-start | bytes 3145728 | tf_op jit(solution)/shard_map/all_to_all | solution.py:418
  260.4 28.5 %collective-permute-start = (bf16[32,128,128]{2,1,0:T(8,128)(2,1)S(1)}, bf16[32,128,128]{2,1,0:T(8,128)(2,1)}, u32[]{:S(2)}, u32[]{:S(2)}) collective-permute-start(bf16[32,128,128]{2,1,0:T(8,128)(2,1)S(1)} %copy-done.8), channel_id=1, source_target_pairs={{0,1},{1,0},{2,3},{3,2},{4,5},{5,4},{6,7},{7,6},{8,9},{9,8},{10,11... | collective-permute-start | bytes 3145736 | tf_op jit(solution)/shard_map/ppermute | solution.py:421
  260.4 30.9 %collective-permute-start.1 = (bf16[32,128,128]{2,1,0:T(8,128)(2,1)}, bf16[32,128,128]{2,1,0:T(8,128)(2,1)}, u32[]{:S(2)}, u32[]{:S(2)}) collective-permute-start(bf16[32,128,128]{2,1,0:T(8,128)(2,1)} %copy-done.11), channel_id=1, source_target_pairs={{0,1},{1,0},{2,3},{3,2},{4,5},{5,4},{6,7},{7,6},{8,9},{9,8},{10,11... | collective-permute-start | bytes 3145736 | tf_op jit(solution)/shard_map/ppermute | solution.py:421
  260.9 34.1 %collective-permute-start.2 = (bf16[32,128,128]{2,1,0:T(8,128)(2,1)}, bf16[32,128,128]{2,1,0:T(8,128)(2,1)}, u32[]{:S(2)}, u32[]{:S(2)}) collective-permute-start(bf16[32,128,128]{2,1,0:T(8,128)(2,1)} %copy-done.9), channel_id=1, source_target_pairs={{0,1},{1,0},{2,3},{3,2},{4,5},{5,4},{6,7},{7,6},{8,9},{9,8},{10,11... | collective-permute-start | bytes 3145736 | tf_op jit(solution)/shard_map/ppermute | solution.py:421
  261.0 1.4 copy-start.16
  283.4 15.0 %collective-permute-start.3 = (bf16[32,128,128]{2,1,0:T(8,128)(2,1)}, bf16[32,128,128]{2,1,0:T(8,128)(2,1)}, u32[]{:S(2)}, u32[]{:S(2)}) collective-permute-start(bf16[32,128,128]{2,1,0:T(8,128)(2,1)} %get-tuple-element.22.mine_ref), channel_id=1, source_target_pairs={{0,1},{1,0},{2,3},{3,2},{4,5},{5,4},{6,7},{7,6},{8,9},{9,8},{10,11... | collective-permute-start | bytes 3145736 | tf_op jit(solution)/shard_map/ppermute | solution.py:421
  288.8 2.5 copy-start.12
  301.8 5.0 %collective-permute-start.4 = (f32[2]{0:T(128)S(1)}, f32[2]{0:T(128)S(1)}, u32[]{:S(2)}, u32[]{:S(2)}) collective-permute-start(f32[2]{0:T(128)S(1)} %pad_maximum_fusion), channel_id=1, source_target_pairs={{0,1},{1,0},{2,3},{3,2},{4,5},{5,4},{6,7},{7,6},{8,9},{9,8},{10,11... | collective-permute-start | bytes 32 | tf_op jit(solution)/shard_map/ppermute | solution.py:190
  301.9 78.5 %all-to-all-start.1 = ((bf16[4,32,48,128]{3,2,1,0:T(8,128)(2,1)}), bf16[4,32,48,128]{3,2,1,0:T(8,128)(2,1)}, u32[]{:S(2)}, u32[]{:S(2)}) async-start(bf16[4,32,48,128]{3,2,1,0:T(8,128)(2,1)} %copy-done.14), calls=%async_computation.1 | async-start | bytes 3145728 | tf_op jit(solution)/shard_map/all_to_all | solution.py:418
  306.9 3.5 collective-permute-start.5
  310.5 22.5 %collective-permute-start.6 = (f32[2]{0:T(128)S(1)}, f32[2]{0:T(128)S(1)}, u32[]{:S(2)}, u32[]{:S(2)}) collective-permute-start(f32[2]{0:T(128)S(1)} %fusion.2), channel_id=1, source_target_pairs={{0,4},{4,0},{8,12},{12,8},{1,5},{5,1},{9,13},{13,9},{2,6},{6,2},{1... | collective-permute-start | bytes 32 | tf_op jit(solution)/shard_map/ppermute | solution.py:190
  333.1 11.5 %collective-permute-start.7 = (f32[2]{0:T(128)S(1)}, f32[2]{0:T(128)S(1)}, u32[]{:S(2)}, u32[]{:S(2)}) collective-permute-start(f32[2]{0:T(128)S(1)} %add.63), channel_id=1, source_target_pairs={{0,8},{4,12},{8,0},{12,4},{1,9},{5,13},{9,1},{13,5},{2,10},{6,14},... | collective-permute-start | bytes 32 | tf_op jit(solution)/shard_map/ppermute | solution.py:190
  346.5 3.8 copy-start.13
  350.3 3.8 copy-start.10
  357.8 4.0 %copy-start.2 = (bf16[512,1024]{1,0:T(8,128)(2,1)S(1)}, bf16[512,1024]{1,0:T(8,128)(2,1)}, u32[]{:S(2)}) copy-start(bf16[512,1024]{1,0:T(8,128)(2,1)} %constant.42.clone.table_ref) | copy-start | bytes 3145732
  361.8 6.2 %copy-start.6 = (bf16[4,32,48,128]{3,2,1,0:T(8,128)(2,1)S(1)}, bf16[4,32,48,128]{3,2,1,0:T(8,128)(2,1)}, u32[]{:S(2)}) copy-start(bf16[4,32,48,128]{3,2,1,0:T(8,128)(2,1)} %copy-done.5) | copy-start | bytes 4718596
  368.0 6.2 %copy-start.4 = (bf16[4,32,48,128]{3,2,1,0:T(8,128)(2,1)S(1)}, bf16[4,32,48,128]{3,2,1,0:T(8,128)(2,1)}, u32[]{:S(2)}) copy-start(bf16[4,32,48,128]{3,2,1,0:T(8,128)(2,1)} %copy-done.3) | copy-start | bytes 4718596
  (8 other events, 8.7 us)

commit v2 on v1

--- a/solution.py
+++ b/solution.py
@@ -424,12 +424,8 @@
         squares.append(jnp.sum(total * total))
 
     sums = jnp.stack([sum(squares) / lax.axis_size("rep"), sum(misfits)])
-    for axis in ("rep", "chan", "lat"):
+    for axis in ("rep", "chan"):
         sums = sum_over(sums, axis)
-    limit = math.sqrt(HIDDEN_FEATURES * K * 2 * L)
-    scale = jnp.minimum(1.0, limit / jnp.sqrt(sums[0] + 1e-06)).reshape(1)
-    total_count = lax.axis_size("rep") * LEADS * HIDDEN_FEATURES * K * 2 * L
-    spectral_misfit = (sums[1] / total_count).reshape(1)
 
     predicted = None
     for chunk in range(CHUNKS):
@@ -446,6 +442,14 @@
             cost(2 * longitude_work, 2 * count * band * span),
             "longitude_inverse",
         )
+        if chunk == CHUNKS - 2:
+            sums, predicted = lax.optimization_barrier((sums, predicted))
+            sums = sum_over(sums, "lat")
+
+    limit = math.sqrt(HIDDEN_FEATURES * K * 2 * L)
+    scale = jnp.minimum(1.0, limit / jnp.sqrt(sums[0] + 1e-06)).reshape(1)
+    total_count = lax.axis_size("rep") * LEADS * HIDDEN_FEATURES * K * 2 * L
+    spectral_misfit = (sums[1] / total_count).reshape(1)
     capped = None
     for chunk in range(CHUNKS):
         capped = chunk_call(

time: 391 us -> 379 us (0.969)
  waiting for transfers between devices: 161 us -> 151 us
  starting transfers between devices: 42.9 us -> 37.8 us
    ppermute x4, waiting for transfers between devices: 29.6 us -> 7.56 us  [sum_over(): lax.ppermute(value, axis, [(i, i ^ step) for i in range(size)])]
    all_to_all x8, waiting for transfers between devices: 132 us -> 143 us  [per_device(): lax.all_to_all(sent, 'lat', split_axis=0, concat_axis=0, tiled=True)]
    ppermute x4, starting transfers between devices: 8.1 us -> 3.61 us  [sum_over(): lax.ppermute(value, axis, [(i, i ^ step) for i in range(size)])]
    unnamed x48 -> x56, local copies, waits for them, and re-layouts: 14 us -> 17.4 us
  transfers between devices with their start and end apart: 16 -> 16, of which waited for: 9 -> 10; matrix products, arithmetic and copies ran while one was open for 3% -> 4% of each run, Pallas kernels for 34% -> 33%
where the time goes in v2:
time: 379 us; the launch traced here: 377 us
  waiting for transfers between devices  151 us (40%)
  Pallas kernels  148 us (39%)
  starting transfers between devices  37.8 us (10%)
  local copies, waits for them, and re-layouts  18.8 us (5%)
  other arithmetic  13.3 us (4%)
  between operations  8.53 us (2%)
    all_to_all x8, waiting for transfers between devices, per_device(): lax.all_to_all(sent, 'lat', split_axis=0, concat_axis=0, tiled=True)  143 us
    pallas_call x4, Pallas kernels, per_device(): pl.pallas_call(rollout_kernel, grid=(steps,), in_specs=[blocked, whole(we...  77.3 us
    pallas_call x8, Pallas kernels, chunk_call(): pl.pallas_call(kernel, grid=(count // group,), in_specs=ins, out_specs=pl...  41 us
    all_to_all x8, starting transfers between devices, per_device(): lax.all_to_all(sent, 'lat', split_axis=0, concat_axis=0, tiled=True)  33.1 us
    pallas_call x4, Pallas kernels, per_device(): pl.pallas_call(forward_kernel, grid=(steps,), in_specs=[pl.BlockSpec((gro...  29.5 us
    unnamed x56, local copies, waits for them, and re-layouts  17.4 us
    reduce_sum x4, other arithmetic, per_device(): squares.append(jnp.sum(total * total))  10.6 us
  transfers between devices with their start and end apart: 16, of which 10 were waited for; matrix products, arithmetic and copies ran while one was open for 4% of the time, Pallas kernels for 33%

profile of v2, /device:TPU:0, one launch (start us, length us, event | category | flops | bytes accessed | tf_op | source)
XLA Modules:
  0.0 377.0 jit_solution(10762148393270646677)
XLA Ops:
  2.7 7.4 %longitude_forward.7 = bf16[4,32,48,128]{3,2,1,0:T(8,128)(2,1)} custom-call(bf16[128,96,1024]{2,1,0:T(8,128)(2,1)} %bitcast.12, bf16[1024,512]{1,0:T(8,128)(2,1)S(1)} %copy-done, bf16[96,96]{1,0:T(8,128)(2,1)S(1)} %copy.17.basis_ref), custom_call_target="tpu_custom_call" | custom-call | flops 6442450944 | bytes 6291456 | tf_op jit(solution)/shard_map/longitude_forward/pallas_call | solution.py:376
  10.1 6.5 %all-to-all-start.4 = ((bf16[4,32,48,128]{3,2,1,0:T(8,128)(2,1)}), bf16[4,32,48,128]{3,2,1,0:T(8,128)(2,1)S(1)}, u32[]{:S(2)}, u32[]{:S(2)}) async-start(bf16[4,32,48,128]{3,2,1,0:T(8,128)(2,1)} %longitude_forward.7), calls=%async_computation.4 | async-start | bytes 3145728 | tf_op jit(solution)/shard_map/all_to_all | solution.py:391
  16.6 7.4 %longitude_forward.6 = bf16[4,32,48,128]{3,2,1,0:T(8,128)(2,1)} custom-call(bf16[128,96,1024]{2,1,0:T(8,128)(2,1)} %bitcast.13, bf16[1024,512]{1,0:T(8,128)(2,1)S(1)} %copy-done.1, bf16[96,96]{1,0:T(8,128)(2,1)S(1)} %copy.17.basis_ref), custom_call_target="tpu_custom_call" | custom-call | flops 6442450944 | bytes 6291456 | tf_op jit(solution)/shard_map/longitude_forward/pallas_call | solution.py:376
  23.9 29.6 %all-to-all-done.4.got_ref = bf16[4,32,48,128]{3,2,1,0:T(8,128)(2,1)S(1)} async-done(((bf16[4,32,48,128]{3,2,1,0:T(8,128)(2,1)}), bf16[4,32,48,128]{3,2,1,0:T(8,128)(2,1)S(1)}, u32[]{:S(2)}, u32[]{:S(2)}) %all-to-all-start.4) | async-done | bytes 1572896 | tf_op jit(solution)/shard_map/all_to_all | solution.py:391
  54.6 3.6 all-to-all-start.3
  58.2 7.4 %longitude_forward.5 = bf16[4,32,48,128]{3,2,1,0:T(8,128)(2,1)} custom-call(bf16[128,96,1024]{2,1,0:T(8,128)(2,1)} %bitcast.14, bf16[1024,512]{1,0:T(8,128)(2,1)S(1)} %copy-done.1, bf16[96,96]{1,0:T(8,128)(2,1)S(1)} %copy.17.basis_ref), custom_call_target="tpu_custom_call" | custom-call | flops 6442450944 | bytes 6291456 | tf_op jit(solution)/shard_map/longitude_forward/pallas_call | solution.py:376
  65.6 29.0 %all-to-all-done.3.got_ref = bf16[4,32,48,128]{3,2,1,0:T(8,128)(2,1)S(1)} async-done(((bf16[4,32,48,128]{3,2,1,0:T(8,128)(2,1)}), bf16[4,32,48,128]{3,2,1,0:T(8,128)(2,1)S(1)}, u32[]{:S(2)}, u32[]{:S(2)}) %all-to-all-start.3) | async-done | bytes 1572896 | tf_op jit(solution)/shard_map/all_to_all | solution.py:391
  95.8 3.6 all-to-all-start.2
  99.4 7.4 %longitude_forward.4 = bf16[4,32,48,128]{3,2,1,0:T(8,128)(2,1)} custom-call(bf16[128,96,1024]{2,1,0:T(8,128)(2,1)} %bitcast.15, bf16[1024,512]{1,0:T(8,128)(2,1)S(1)} %copy-done.1, bf16[96,96]{1,0:T(8,128)(2,1)S(1)} %copy.17.basis_ref), custom_call_target="tpu_custom_call" | custom-call | flops 6442450944 | bytes 6291456 | tf_op jit(solution)/shard_map/longitude_forward/pallas_call | solution.py:376
  106.8 29.0 %all-to-all-done.2.got_ref = bf16[4,32,48,128]{3,2,1,0:T(8,128)(2,1)S(1)} async-done(((bf16[4,32,48,128]{3,2,1,0:T(8,128)(2,1)}), bf16[4,32,48,128]{3,2,1,0:T(8,128)(2,1)S(1)}, u32[]{:S(2)}, u32[]{:S(2)}) %all-to-all-start.2) | async-done | bytes 1572896 | tf_op jit(solution)/shard_map/all_to_all | solution.py:391
  137.0 3.7 all-to-all-start
  140.7 19.2 %rollout.7 = (bf16[4,32,48,128]{3,2,1,0:T(8,128)(2,1)S(1)}, bf16[32,128,128]{2,1,0:T(8,128)(2,1)S(1)}, f32[8,128]{1,0:T(8,128)S(1)}) custom-call(bf16[4,32,48,128]{3,2,1,0:T(8,128)(2,1)S(1)} %copy-done.23, bf16[192,256]{1,0:T(8,128)(2,1)S(1)} %copy-done.26, bf16[128,128]{1,0:T(8,128)(2,1)S(1)} %copy-done.27, f32[128,128,128]{2,1,0:T(8,128)} %bitcast.22, ...), custom_call_target="tpu_custom_call" | custom-call | flops 9663676416 | bytes 10485760 | tf_op jit(solution)/shard_map/rollout/pallas_call | solution.py:396
  162.0 15.1 %all-to-all-done.got_ref = bf16[4,32,48,128]{3,2,1,0:T(8,128)(2,1)S(1)} async-done(((bf16[4,32,48,128]{3,2,1,0:T(8,128)(2,1)}), bf16[4,32,48,128]{3,2,1,0:T(8,128)(2,1)S(1)}, u32[]{:S(2)}, u32[]{:S(2)}) %all-to-all-start) | async-done | bytes 1572896 | tf_op jit(solution)/shard_map/all_to_all | solution.py:391
  178.2 3.6 all-to-all-start.5
  181.8 19.2 %rollout.6 = (bf16[4,32,48,128]{3,2,1,0:T(8,128)(2,1)S(1)}, bf16[32,128,128]{2,1,0:T(8,128)(2,1)S(1)}, f32[8,128]{1,0:T(8,128)S(1)}) custom-call(bf16[4,32,48,128]{3,2,1,0:T(8,128)(2,1)S(1)} %copy-done.21, bf16[192,256]{1,0:T(8,128)(2,1)S(1)} %copy-done.26, bf16[128,128]{1,0:T(8,128)(2,1)S(1)} %copy-done.27, f32[128,128,128]{2,1,0:T(8,128)} %bitcast.23, ...), custom_call_target="tpu_custom_call" | custom-call | flops 9663676416 | bytes 10485760 | tf_op jit(solution)/shard_map/rollout/pallas_call | solution.py:396
  203.1 15.1 %all-to-all-done.5.got_ref = bf16[4,32,48,128]{3,2,1,0:T(8,128)(2,1)S(1)} async-done(((bf16[4,32,48,128]{3,2,1,0:T(8,128)(2,1)}), bf16[4,32,48,128]{3,2,1,0:T(8,128)(2,1)S(1)}, u32[]{:S(2)}, u32[]{:S(2)}) %all-to-all-start.5) | async-done | bytes 1572896 | tf_op jit(solution)/shard_map/all_to_all | solution.py:418
  218.2 3.6 all-to-all-start.6
  223.2 19.1 %rollout.5 = (bf16[4,32,48,128]{3,2,1,0:T(8,128)(2,1)S(1)}, bf16[32,128,128]{2,1,0:T(8,128)(2,1)S(1)}, f32[8,128]{1,0:T(8,128)S(1)}) custom-call(bf16[4,32,48,128]{3,2,1,0:T(8,128)(2,1)S(1)} %copy-done.19, bf16[192,256]{1,0:T(8,128)(2,1)S(1)} %copy-done.26, bf16[128,128]{1,0:T(8,128)(2,1)S(1)} %copy-done.27, f32[128,128,128]{2,1,0:T(8,128)} %bitcast.24, ...), custom_call_target="tpu_custom_call" | custom-call | flops 9663676416 | bytes 10485760 | tf_op jit(solution)/shard_map/rollout/pallas_call | solution.py:396
  244.4 13.8 %all-to-all-done.6.got_ref = bf16[4,32,48,128]{3,2,1,0:T(8,128)(2,1)S(1)} async-done(((bf16[4,32,48,128]{3,2,1,0:T(8,128)(2,1)}), bf16[4,32,48,128]{3,2,1,0:T(8,128)(2,1)S(1)}, u32[]{:S(2)}, u32[]{:S(2)}) %all-to-all-start.6) | async-done | bytes 1572896 | tf_op jit(solution)/shard_map/all_to_all | solution.py:418
  259.4 3.7 all-to-all-start.7
  265.1 19.8 %rollout.4 = (bf16[4,32,48,128]{3,2,1,0:T(8,128)(2,1)S(1)}, bf16[32,128,128]{2,1,0:T(8,128)(2,1)}, f32[8,128]{1,0:T(8,128)S(1)}) custom-call(bf16[4,32,48,128]{3,2,1,0:T(8,128)(2,1)S(1)} %copy-done.17, bf16[192,256]{1,0:T(8,128)(2,1)S(1)} %copy-done.26, bf16[128,128]{1,0:T(8,128)(2,1)S(1)} %copy-done.27, f32[128,128,128]{2,1,0:T(8,128)} %bitcast.25, ...), custom_call_target="tpu_custom_call" | custom-call | flops 9663676416 | bytes 10485760 | tf_op jit(solution)/shard_map/rollout/pallas_call | solution.py:396
  304.8 5.0 %all-to-all-start.1 = ((bf16[4,32,48,128]{3,2,1,0:T(8,128)(2,1)}), bf16[4,32,48,128]{3,2,1,0:T(8,128)(2,1)}, u32[]{:S(2)}, u32[]{:S(2)}) async-start(bf16[4,32,48,128]{3,2,1,0:T(8,128)(2,1)} %copy-done.14), calls=%async_computation.1 | async-start | bytes 3145728 | tf_op jit(solution)/shard_map/all_to_all | solution.py:418
  314.7 6.2 %longitude_inverse.4.refs_0_ = bf16[128,96,1024]{2,1,0:T(8,128)(2,1)} custom-call(bf16[4,32,48,128]{3,2,1,0:T(8,128)(2,1)S(1)} %all-to-all-done.7.got_ref, bf16[96,96]{1,0:T(8,128)(2,1)S(1)} %get-tuple-element.31.basis_ref, bf16[512,1024]{1,0:T(8,128)(2,1)S(1)} %copy-done.2), custom_call_target="tpu_custom_call" | custom-call | flops 6442450944 | bytes 6291456 | tf_op jit(solution)/shard_map/longitude_inverse/pallas_call | solution.py:327
  321.0 6.2 %longitude_inverse.5.refs_0_ = bf16[128,96,1024]{2,1,0:T(8,128)(2,1)} custom-call(bf16[4,32,48,128]{3,2,1,0:T(8,128)(2,1)S(1)} %copy-done.6, bf16[96,96]{1,0:T(8,128)(2,1)S(1)} %get-tuple-element.31.basis_ref, bf16[512,1024]{1,0:T(8,128)(2,1)S(1)} %copy-done.2, bf16[128,96,1024]{2,1,0:T(8,128)(2,1)} %longitude_inverse.4.refs_0_), custom_call_target="tpu_custom_call", output_to_operand_aliasing={{}: (3, {})} | custom-call | flops 6442450944 | bytes 6291456 | tf_op jit(solution)/shard_map/longitude_inverse/pallas_call | solution.py:327
  327.2 6.2 %longitude_inverse.6.refs_0_ = bf16[128,96,1024]{2,1,0:T(8,128)(2,1)} custom-call(bf16[4,32,48,128]{3,2,1,0:T(8,128)(2,1)S(1)} %copy-done.4, bf16[96,96]{1,0:T(8,128)(2,1)S(1)} %get-tuple-element.31.basis_ref, bf16[512,1024]{1,0:T(8,128)(2,1)S(1)} %copy-done.2, bf16[128,96,1024]{2,1,0:T(8,128)(2,1)} %longitude_inverse.5.refs_0_), custom_call_target="tpu_custom_call", output_to_operand_aliasing={{}: (3, {})} | custom-call | flops 6442450944 | bytes 6291456 | tf_op jit(solution)/shard_map/longitude_inverse/pallas_call | solution.py:327
  335.4 11.7 %all-to-all-done.1.got_ref = bf16[4,32,48,128]{3,2,1,0:T(8,128)(2,1)} async-done(((bf16[4,32,48,128]{3,2,1,0:T(8,128)(2,1)}), bf16[4,32,48,128]{3,2,1,0:T(8,128)(2,1)}, u32[]{:S(2)}, u32[]{:S(2)}) %all-to-all-start.1) | async-done | bytes 1572896 | tf_op jit(solution)/shard_map/all_to_all | solution.py:418
  347.1 7.2 %longitude_inverse.7 = bf16[128,96,1024]{2,1,0:T(8,128)(2,1)} custom-call(bf16[4,32,48,128]{3,2,1,0:T(8,128)(2,1)} %all-to-all-done.1.got_ref, bf16[96,96]{1,0:T(8,128)(2,1)S(1)} %get-tuple-element.31.basis_ref, bf16[512,1024]{1,0:T(8,128)(2,1)S(1)} %copy-done.2, bf16[128,96,1024]{2,1,0:T(8,128)(2,1)} %longitude_inverse.6.refs_0_), custom_call_target="tpu_custom_call", output_to_operand_aliasing={{}: (3, {})} | custom-call | flops 6442450944 | bytes 6291456 | tf_op jit(solution)/shard_map/longitude_inverse/pallas_call | solution.py:327
  354.3 4.4 %collective-permute-done.7 = f32[2]{0:T(128)S(1)} collective-permute-done((f32[2]{0:T(128)S(1)}, f32[2]{0:T(128)S(1)}, u32[]{:S(2)}, u32[]{:S(2)}) %collective-permute-start.7) | collective-permute-done | bytes 40 | tf_op jit(solution)/shard_map/ppermute | solution.py:190
  360.7 3.8 %scale.4.refs_0_ = f32[128,128,128]{2,1,0:T(8,128)} custom-call(f32[1]{0:T(128)S(6)} %min_shard_map.4.scale_ref, bf16[32,128,128]{2,1,0:T(8,128)(2,1)S(1)} %copy-done.9, bf16[32,128,128]{2,1,0:T(8,128)(2,1)} %collective-permute-done.other_ref), custom_call_target="tpu_custom_call" | custom-call | flops 2097152 | bytes 4194304 | tf_op jit(solution)/shard_map/scale/pallas_call | solution.py:327
  364.5 3.8 %scale.5.refs_0_ = f32[128,128,128]{2,1,0:T(8,128)} custom-call(f32[1]{0:T(128)S(6)} %min_shard_map.4.scale_ref, bf16[32,128,128]{2,1,0:T(8,128)(2,1)S(1)} %copy-done.13, bf16[32,128,128]{2,1,0:T(8,128)(2,1)} %collective-permute-done.1.other_ref, f32[128,128,128]{2,1,0:T(8,128)} %scale.4.refs_0_), custom_call_target="tpu_custom_call", output_to_operand_aliasing={{}: (3, {})} | custom-call | flops 2097152 | bytes 4194304 | tf_op jit(solution)/shard_map/scale/pallas_call | solution.py:327
  368.3 3.7 scale.6.refs_0_
  372.0 3.9 %scale.7 = f32[128,128,128]{2,1,0:T(8,128)} custom-call(f32[1]{0:T(128)S(6)} %min_shard_map.4.scale_ref, bf16[32,128,128]{2,1,0:T(8,128)(2,1)} %get-tuple-element.21.mine_ref, bf16[32,128,128]{2,1,0:T(8,128)(2,1)} %collective-permute-done.3.other_ref, f32[128,128,128]{2,1,0:T(8,128)} %scale.6.refs_0_), custom_call_target="tpu_custom_call", output_to_operand_aliasing={{}: (3, {})} | custom-call | flops 2097152 | bytes 4194304 | tf_op jit(solution)/shard_map/scale/pallas_call | solution.py:327
  (88 shorter events, 40.0 us)
Async XLA Ops:
  1.5 1.2 copy-start
  10.1 6.5 %copy-start.1 = (bf16[1024,512]{1,0:T(8,128)(2,1)S(1)}, bf16[1024,512]{1,0:T(8,128)(2,1)}, u32[]{:S(2)}) copy-start(bf16[1024,512]{1,0:T(8,128)(2,1)} %constant.41.clone.table_ref) | copy-start | bytes 3145732
  10.1 43.4 %all-to-all-start.4 = ((bf16[4,32,48,128]{3,2,1,0:T(8,128)(2,1)}), bf16[4,32,48,128]{3,2,1,0:T(8,128)(2,1)S(1)}, u32[]{:S(2)}, u32[]{:S(2)}) async-start(bf16[4,32,48,128]{3,2,1,0:T(8,128)(2,1)} %longitude_forward.7), calls=%async_computation.4 | async-start | bytes 3145728 | tf_op jit(solution)/shard_map/all_to_all | solution.py:391
  54.6 40.0 %all-to-all-start.3 = ((bf16[4,32,48,128]{3,2,1,0:T(8,128)(2,1)}), bf16[4,32,48,128]{3,2,1,0:T(8,128)(2,1)S(1)}, u32[]{:S(2)}, u32[]{:S(2)}) async-start(bf16[4,32,48,128]{3,2,1,0:T(8,128)(2,1)} %longitude_forward.6), calls=%async_computation.3 | async-start | bytes 3145728 | tf_op jit(solution)/shard_map/all_to_all | solution.py:391
  95.8 40.0 %all-to-all-start.2 = ((bf16[4,32,48,128]{3,2,1,0:T(8,128)(2,1)}), bf16[4,32,48,128]{3,2,1,0:T(8,128)(2,1)S(1)}, u32[]{:S(2)}, u32[]{:S(2)}) async-start(bf16[4,32,48,128]{3,2,1,0:T(8,128)(2,1)} %longitude_forward.5), calls=%async_computation.2 | async-start | bytes 3145728 | tf_op jit(solution)/shard_map/all_to_all | solution.py:391
  106.8 33.9 %copy-start.26 = (bf16[192,256]{1,0:T(8,128)(2,1)S(1)}, bf16[192,256]{1,0:T(8,128)(2,1)}, u32[]{:S(2)}) copy-start(bf16[192,256]{1,0:T(8,128)(2,1)} %constant.40.clone.weights_ref) | copy-start | bytes 294916
  106.8 33.9 %copy-start.27 = (bf16[128,128]{1,0:T(8,128)(2,1)S(1)}, bf16[128,128]{1,0:T(8,128)(2,1)}, u32[]{:S(2)}) copy-start(bf16[128,128]{1,0:T(8,128)(2,1)} %constant.43.clone.order_ref) | copy-start | bytes 98308
  137.0 3.7 copy-start.23
  137.0 40.1 %all-to-all-start = ((bf16[4,32,48,128]{3,2,1,0:T(8,128)(2,1)}), bf16[4,32,48,128]{3,2,1,0:T(8,128)(2,1)S(1)}, u32[]{:S(2)}, u32[]{:S(2)}) async-start(bf16[4,32,48,128]{3,2,1,0:T(8,128)(2,1)} %longitude_forward.4), calls=%async_computation | async-start | bytes 3145728 | tf_op jit(solution)/shard_map/all_to_all | solution.py:391
  162.0 19.8 %copy-start.21 = (bf16[4,32,48,128]{3,2,1,0:T(8,128)(2,1)S(1)}, bf16[4,32,48,128]{3,2,1,0:T(8,128)(2,1)}, u32[]{:S(2)}) copy-start(bf16[4,32,48,128]{3,2,1,0:T(8,128)(2,1)} %copy-done.20) | copy-start | bytes 4718596
  178.2 40.0 %all-to-all-start.5 = ((bf16[4,32,48,128]{3,2,1,0:T(8,128)(2,1)}), bf16[4,32,48,128]{3,2,1,0:T(8,128)(2,1)S(1)}, u32[]{:S(2)}, u32[]{:S(2)}) async-start(bf16[4,32,48,128]{3,2,1,0:T(8,128)(2,1)} %copy-done.24), calls=%async_computation.5 | async-start | bytes 3145728 | tf_op jit(solution)/shard_map/all_to_all | solution.py:418
  218.2 24.1 %copy-start.3 = (bf16[4,32,48,128]{3,2,1,0:T(8,128)(2,1)}, bf16[4,32,48,128]{3,2,1,0:T(8,128)(2,1)S(1)}, u32[]{:S(2)}) copy-start(bf16[4,32,48,128]{3,2,1,0:T(8,128)(2,1)S(1)} %all-to-all-done.5.got_ref) | copy-start | bytes 4718596
  218.2 40.0 %all-to-all-start.6 = ((bf16[4,32,48,128]{3,2,1,0:T(8,128)(2,1)}), bf16[4,32,48,128]{3,2,1,0:T(8,128)(2,1)S(1)}, u32[]{:S(2)}, u32[]{:S(2)}) async-start(bf16[4,32,48,128]{3,2,1,0:T(8,128)(2,1)} %copy-done.25), calls=%async_computation.6 | async-start | bytes 3145728 | tf_op jit(solution)/shard_map/all_to_all | solution.py:418
  221.8 1.4 copy-start.19
  259.4 4.3 %copy-start.8 = (bf16[32,128,128]{2,1,0:T(8,128)(2,1)S(1)}, bf16[32,128,128]{2,1,0:T(8,128)(2,1)}, u32[]{:S(2)}) copy-start(bf16[32,128,128]{2,1,0:T(8,128)(2,1)} %copy-done.7) | copy-start | bytes 3145732
  259.4 45.5 %all-to-all-start.7 = ((bf16[4,32,48,128]{3,2,1,0:T(8,128)(2,1)}), bf16[4,32,48,128]{3,2,1,0:T(8,128)(2,1)S(1)}, u32[]{:S(2)}, u32[]{:S(2)}) async-start(bf16[4,32,48,128]{3,2,1,0:T(8,128)(2,1)} %copy-done.15), calls=%async_computation.7 | async-start | bytes 3145728 | tf_op jit(solution)/shard_map/all_to_all | solution.py:418
  263.1 35.0 %collective-permute-start.2 = (bf16[32,128,128]{2,1,0:T(8,128)(2,1)}, bf16[32,128,128]{2,1,0:T(8,128)(2,1)}, u32[]{:S(2)}, u32[]{:S(2)}) collective-permute-start(bf16[32,128,128]{2,1,0:T(8,128)(2,1)} %copy-done.10), channel_id=1, source_target_pairs={{0,1},{1,0},{2,3},{3,2},{4,5},{5,4},{6,7},{7,6},{8,9},{9,8},{10,11... | collective-permute-start | bytes 3145736 | tf_op jit(solution)/shard_map/ppermute | solution.py:421
  263.1 28.5 %collective-permute-start.1 = (bf16[32,128,128]{2,1,0:T(8,128)(2,1)}, bf16[32,128,128]{2,1,0:T(8,128)(2,1)}, u32[]{:S(2)}, u32[]{:S(2)}) collective-permute-start(bf16[32,128,128]{2,1,0:T(8,128)(2,1)} %copy-done.12), channel_id=1, source_target_pairs={{0,1},{1,0},{2,3},{3,2},{4,5},{5,4},{6,7},{7,6},{8,9},{9,8},{10,11... | collective-permute-start | bytes 3145736 | tf_op jit(solution)/shard_map/ppermute | solution.py:421
  263.6 30.8 %collective-permute-start = (bf16[32,128,128]{2,1,0:T(8,128)(2,1)S(1)}, bf16[32,128,128]{2,1,0:T(8,128)(2,1)}, u32[]{:S(2)}, u32[]{:S(2)}) collective-permute-start(bf16[32,128,128]{2,1,0:T(8,128)(2,1)S(1)} %copy-done.8), channel_id=1, source_target_pairs={{0,1},{1,0},{2,3},{3,2},{4,5},{5,4},{6,7},{7,6},{8,9},{9,8},{10,11... | collective-permute-start | bytes 3145736 | tf_op jit(solution)/shard_map/ppermute | solution.py:421
  263.7 1.4 copy-start.17
  286.1 15.3 %collective-permute-start.3 = (bf16[32,128,128]{2,1,0:T(8,128)(2,1)}, bf16[32,128,128]{2,1,0:T(8,128)(2,1)}, u32[]{:S(2)}, u32[]{:S(2)}) collective-permute-start(bf16[32,128,128]{2,1,0:T(8,128)(2,1)} %get-tuple-element.21.mine_ref), channel_id=1, source_target_pairs={{0,1},{1,0},{2,3},{3,2},{4,5},{5,4},{6,7},{7,6},{8,9},{9,8},{10,11... | collective-permute-start | bytes 3145736 | tf_op jit(solution)/shard_map/ppermute | solution.py:421
  304.1 10.6 %copy-start.2 = (bf16[512,1024]{1,0:T(8,128)(2,1)S(1)}, bf16[512,1024]{1,0:T(8,128)(2,1)}, u32[]{:S(2)}) copy-start(bf16[512,1024]{1,0:T(8,128)(2,1)} %constant.42.clone.table_ref) | copy-start | bytes 3145732
  304.8 42.3 %all-to-all-start.1 = ((bf16[4,32,48,128]{3,2,1,0:T(8,128)(2,1)}), bf16[4,32,48,128]{3,2,1,0:T(8,128)(2,1)}, u32[]{:S(2)}, u32[]{:S(2)}) async-start(bf16[4,32,48,128]{3,2,1,0:T(8,128)(2,1)} %copy-done.14), calls=%async_computation.1 | async-start | bytes 3145728 | tf_op jit(solution)/shard_map/all_to_all | solution.py:418
  309.9 1.1 collective-permute-start.4
  311.1 3.5 collective-permute-start.5
  314.7 6.2 %copy-start.6 = (bf16[4,32,48,128]{3,2,1,0:T(8,128)(2,1)S(1)}, bf16[4,32,48,128]{3,2,1,0:T(8,128)(2,1)}, u32[]{:S(2)}) copy-start(bf16[4,32,48,128]{3,2,1,0:T(8,128)(2,1)} %copy-done.5) | copy-start | bytes 4718596
  321.0 6.2 %copy-start.4 = (bf16[4,32,48,128]{3,2,1,0:T(8,128)(2,1)S(1)}, bf16[4,32,48,128]{3,2,1,0:T(8,128)(2,1)}, u32[]{:S(2)}) copy-start(bf16[4,32,48,128]{3,2,1,0:T(8,128)(2,1)} %copy-done.3) | copy-start | bytes 4718596
  333.4 27.3 %copy-start.9 = (bf16[32,128,128]{2,1,0:T(8,128)(2,1)S(1)}, bf16[32,128,128]{2,1,0:T(8,128)(2,1)}, u32[]{:S(2)}) copy-start(bf16[32,128,128]{2,1,0:T(8,128)(2,1)} %copy-done.7) | copy-start | bytes 3145732
  333.4 20.9 %collective-permute-start.6 = (f32[2]{0:T(128)S(1)}, f32[2]{0:T(128)S(1)}, u32[]{:S(2)}, u32[]{:S(2)}) collective-permute-start(f32[2]{0:T(128)S(1)} %fusion.2), channel_id=1, source_target_pairs={{0,4},{4,0},{8,12},{12,8},{1,5},{5,1},{9,13},{13,9},{2,6},{6,2},{1... | collective-permute-start | bytes 32 | tf_op jit(solution)/shard_map/ppermute | solution.py:190
  354.3 4.5 %collective-permute-start.7 = (f32[2]{0:T(128)S(1)}, f32[2]{0:T(128)S(1)}, u32[]{:S(2)}, u32[]{:S(2)}) collective-permute-start(f32[2]{0:T(128)S(1)} %add.63), channel_id=1, source_target_pairs={{0,8},{4,12},{8,0},{12,4},{1,9},{5,13},{9,1},{13,5},{2,10},{6,14},... | collective-permute-start | bytes 32 | tf_op jit(solution)/shard_map/ppermute | solution.py:190
  360.7 3.8 %copy-start.13 = (bf16[32,128,128]{2,1,0:T(8,128)(2,1)S(1)}, bf16[32,128,128]{2,1,0:T(8,128)(2,1)}, u32[]{:S(2)}) copy-start(bf16[32,128,128]{2,1,0:T(8,128)(2,1)} %copy-done.12) | copy-start | bytes 3145732
  364.5 3.8 %copy-start.11 = (bf16[32,128,128]{2,1,0:T(8,128)(2,1)S(1)}, bf16[32,128,128]{2,1,0:T(8,128)(2,1)}, u32[]{:S(2)}) copy-start(bf16[32,128,128]{2,1,0:T(8,128)(2,1)} %copy-done.10) | copy-start | bytes 3145732
  (12 other events, 13.3 us)
